TPU v7x, 128 devices: a whole 4x4x4 slice. The times are simulated.
128 devices in a mesh: row: 8 (over x, core), col: 16 (over y, z).
Axes of the slice: x: 4, y: 4, z: 4, core: 2. Of those that a mesh axis runs over, the one named last changes fastest.
Arguments:
- query_single: bfloat16 [1024, 384], P('row', 'col'), may hold values from -18 to 18
- query_rotation: float32 [9, 1024], P(None, 'row'), may hold values from -1 to 1, as said below
- query_anchor: float32 [3, 1024], P(None, 'row'), may hold values from -5 to 5
- query_chain: int32 [1024], P('row'), may hold values from 0 to 15, never falling along the last dimension, each value on 1 to 128 neighbouring positions
- key_single: bfloat16 [8192, 384], P(('col', 'row')), may hold values from -5 to 5
- key_rotation: float32 [9, 8192], P(None, ('col', 'row')), may hold values from -1 to 1, as said below
- key_anchor: float32 [3, 8192], P(None, ('col', 'row')), may hold values from -5 to 5
- key_chain: int32 [8192], P('col'), may hold values from 0 to 15, never falling along the last dimension, each value on 1 to 1024 neighbouring positions
- key_mask: int32 [8192], P('col'), may hold values 0 or 1
- pair_tile: bfloat16 [1024, 8192, 128], P('row', 'col'), may hold values from -50 to 50
- query_weight: bfloat16 [384, 192], replicated, may hold values from -0.3125 to 0.3125
- query_point_weight: bfloat16 [384, 144], replicated, may hold values from -0.3125 to 0.3125
- key_weight: bfloat16 [384, 192], replicated, may hold values from -0.3125 to 0.3125
- value_weight: bfloat16 [384, 192], replicated, may hold values from -0.3125 to 0.3125
- key_point_weight: bfloat16 [384, 144], replicated, may hold values from -0.3125 to 0.3125
- value_point_weight: bfloat16 [384, 288], replicated, may hold values from -0.3125 to 0.3125
- pair_weight: bfloat16 [128, 12], replicated, may hold values from -1 to 1
- head_gamma: float32 [12], replicated, may hold values from 0.05 to 1
- chain_gap: float32 [12], replicated, may hold values from -3 to 3
- out_weight: bfloat16 [2016, 384], P(None, 'col'), may hold values from -1 to 1
- norm_gain: float32 [384], P('col'), may hold values from 0.1 to 1.9
- norm_shift: float32 [384], P('col'), may hold values from -3 to 3
Outputs:
- updated_single: bfloat16 [1024, 384], P('row', 'col')
Inputs may be any that keep to these rules, and one draw needn't show every extreme that they name: `query_rotation`: each column of 9 is a rotation matrix. `key_rotation`: each column of 9 is a rotation matrix. `query_chain`: ids never fall along the query residues. `key_chain`: ids never fall along the residues.
All inputs are finite; a program needn't handle non-finite values. No bound on the sum of `key_mask` on one device may be relied on, other than what follows from the above.
Results may differ from a plain program's by a relative error of at most 0.0095.
Values may be sent and summed in bfloat16 or wider, within the bound.
No kernel may reach another device: no remote copies, remote signals or barrier semaphores. Data moves between devices by JAX's collectives and lax.ppermute only.
A program may use at most 128 MiB of HBM per device.

v0:
```python
import jax
import jax.numpy as jnp
from jax import lax
from jax.sharding import PartitionSpec as P

D = 384
H = 12
C = 16
PQ = 4
PV = 8
FEAT = 168


LOGIT_SCALE = (1.0 / 3.0) ** 0.5
NORM_EPS = 1e-05
MASKED = -1000000000.0
PRECISE = lax.Precision.HIGHEST


def rotate(rotation, local_points, translation):
    moved = []
    for component in range(3):
        moved.append(
            rotation[3 * component] * local_points[0]
            + rotation[3 * component + 1] * local_points[1]
            + rotation[3 * component + 2] * local_points[2]
            + translation[component]
        )
    return jnp.stack(moved)


def key_package(
    residues, rotation, translation, key_weight, value_weight, key_point_weight, value_point_weight
):
    residue_count = residues.shape[0]
    weights = jnp.concatenate(
        [key_weight, value_weight, key_point_weight, value_point_weight], axis=1
    )
    projected = jnp.dot(residues, weights, preferred_element_type=jnp.float32).T
    first_cut = 2 * H * C
    second_cut = first_cut + 3 * H * PQ
    key_points = rotate(
        rotation, projected[first_cut:second_cut].reshape(3, H * PQ, residue_count), translation
    )
    value_points = rotate(
        rotation, projected[second_cut:].reshape(3, H * PV, residue_count), translation
    )
    return jnp.concatenate(
        [
            projected[:first_cut],
            key_points.reshape(3 * H * PQ, residue_count),
            value_points.reshape(3 * H * PV, residue_count),
        ],
        axis=0,
    ).astype(jnp.bfloat16)


def block_partials(
    queries,
    query_points,
    query_chain,
    package,
    key_chain,
    key_mask,
    pair,
    pair_weight,
    head_gamma,
    chain_gap,
):
    key_count = package.shape[1]
    query_count = queries.shape[2]
    first_cut = 2 * H * C
    second_cut = first_cut + 3 * H * PQ
    keys_block = package[: H * C].reshape(H, C, key_count)
    values_block = package[H * C : first_cut].reshape(H, C, key_count)
    key_points = package[first_cut:second_cut].astype(jnp.float32).reshape(3, H, PQ, key_count)
    value_points = package[second_cut:].reshape(3, H, PV, key_count)
    affinity = jnp.einsum("hcq,hck->hqk", queries, keys_block, preferred_element_type=jnp.float32)
    pair_bias = jnp.einsum("qkc,ch->hqk", pair, pair_weight, preferred_element_type=jnp.float32)
    inner_products = jnp.einsum("ahpq,ahpk->hqk", query_points, key_points, precision=PRECISE)
    query_norms = jnp.sum(query_points * query_points, axis=(0, 2))
    key_norms = jnp.sum(key_points * key_points, axis=(0, 2))
    distances = query_norms[:, :, None] + key_norms[:, None, :] - 2.0 * inner_products
    chain_apart = (query_chain[:, None] != key_chain[None, :]).astype(jnp.float32)
    point_scale = head_gamma * (2.0 / (9.0 * PQ)) ** 0.5 * 0.5
    logits = LOGIT_SCALE * (
        affinity * C ** (-0.5)
        + pair_bias
        + chain_gap[:, None, None] * chain_apart[None]
        - point_scale[:, None, None] * distances
    )
    logits = jnp.where(key_mask[None, None, :] > 0, logits, MASKED)
    maximum = jnp.max(logits, axis=-1)
    attention = jnp.exp(logits - maximum[:, :, None]).astype(jnp.bfloat16)
    weight_sum = jnp.sum(attention, axis=-1, dtype=jnp.float32)
    value_part = jnp.einsum(
        "hqk,hck->hcq", attention, values_block, preferred_element_type=jnp.float32
    )
    point_part = jnp.einsum(
        "hqk,ahpk->hapq", attention, value_points, preferred_element_type=jnp.float32
    ).reshape(H, 3 * PV, query_count)
    pair_part = jnp.einsum("hqk,qkc->hcq", attention, pair, preferred_element_type=jnp.float32)
    return (maximum, weight_sum, jnp.concatenate([value_part, point_part, pair_part], axis=1))


def finish(weight_sum, numerators, rotation, translation):
    averaged = numerators / weight_sum[:, None, :]
    global_points = averaged[:, C : C + 3 * PV].reshape(H, 3, PV, -1)
    shifted = global_points - translation[None, :, None, :]
    local_list = []
    for component in range(3):
        local_list.append(
            rotation[component] * shifted[:, 0]
            + rotation[3 + component] * shifted[:, 1]
            + rotation[6 + component] * shifted[:, 2]
        )
    local_points = jnp.stack(local_list, axis=1).reshape(H, 3 * PV, -1)
    joined = jnp.concatenate([averaged[:, :C], local_points, averaged[:, C + 3 * PV :]], axis=1)
    return joined.reshape(H * FEAT, -1).astype(jnp.bfloat16)


def on_device(
    query_single,
    query_rotation,
    query_anchor,
    query_chain,
    key_single,
    key_rotation,
    key_anchor,
    key_chain,
    key_mask,
    pair_tile,
    query_weight,
    query_point_weight,
    key_weight,
    value_weight,
    key_point_weight,
    value_point_weight,
    pair_weight,
    head_gamma,
    chain_gap,
    out_weight,
    norm_gain,
    norm_shift,
):
    full_rows = lax.all_gather(query_single, "col", axis=1, tiled=True)
    query_count = full_rows.shape[0]
    projected = jnp.dot(
        full_rows,
        jnp.concatenate([query_weight, query_point_weight], axis=1),
        preferred_element_type=jnp.float32,
    ).T
    queries = projected[: H * C].astype(jnp.bfloat16).reshape(H, C, query_count)
    query_points = rotate(
        query_rotation, projected[H * C :].reshape(3, H * PQ, query_count), query_anchor
    ).reshape(3, H, PQ, query_count)
    own_rows = key_package(
        key_single,
        key_rotation,
        key_anchor,
        key_weight,
        value_weight,
        key_point_weight,
        value_point_weight,
    )
    package = lax.all_gather(own_rows, "row", axis=1, tiled=True)
    maximum, weight_sum, numerators = block_partials(
        queries,
        query_points,
        query_chain,
        package,
        key_chain,
        key_mask,
        pair_tile,
        pair_weight,
        head_gamma,
        chain_gap,
    )
    highest = lax.pmax(maximum, "col")
    factor = jnp.exp(maximum - highest)
    weight_sum, numerators = (
        lax.psum((weight_sum * factor).astype(jnp.bfloat16), "col").astype(jnp.float32),
        lax.psum((numerators * factor[:, None, :]).astype(jnp.bfloat16), "col").astype(jnp.float32),
    )
    features = finish(weight_sum, numerators, query_rotation, query_anchor)
    mixed = query_single.astype(jnp.float32) + jnp.dot(
        features.T, out_weight, preferred_element_type=jnp.float32
    )
    average = lax.psum(jnp.sum(mixed, axis=1), "col") / D
    centred = mixed - average[:, None]
    variance = lax.psum(jnp.sum(centred * centred, axis=1), "col") / D
    return (centred * lax.rsqrt(variance + NORM_EPS)[:, None] * norm_gain + norm_shift).astype(
        jnp.bfloat16
    )


def solution(mesh):
    placed = (
        P("row", "col"),
        P(None, "row"),
        P(None, "row"),
        P("row"),
        P(("col", "row"), None),
        P(None, ("col", "row")),
        P(None, ("col", "row")),
        P("col"),
        P("col"),
        P("row", "col", None),
        P(),
        P(),
        P(),
        P(),
        P(),
        P(),
        P(),
        P(),
        P(),
        P(None, "col"),
        P("col"),
        P("col"),
    )
    return jax.shard_map(
        on_device, mesh=mesh, in_specs=placed, out_specs=P("row", "col"), check_vma=False
    )
```

profile of v0, /device:TPU:0, one launch (start us, length us, event | category | flops | bytes accessed | tf_op | source)
XLA Modules:
  0.0 296.1 jit_solution(273604998658349336)
XLA Ops:
  6.5 1.0 slice_bitcast_fusion.21
  7.5 1.5 fusion.17
  9.1 0.1 fusion.37
  9.2 0.1 fusion.34
  9.3 0.2 fusion.32
  9.5 0.2 fusion.35
  9.7 0.1 copy.87
  9.8 0.1 copy.89
  10.0 0.1 reshape.116
  10.1 0.1 pad_maximum_fusion.1
  10.2 14.0 %all_gather.6 = bf16[816,512]{0,1:T(8,128)(2,1)S(1)} all-gather(bf16[816,64]{0,1:T(8,128)(2,1)S(1)} %pad_maximum_fusion.1), channel_id=1, replica_groups=mesh['row'=8,'col'=16] {'row'}, dimensions={1}, use_global_device_ids=true | all-gather | bytes 940032 | tf_op jit(solution)/shard_map/all_gather | solution.py:166
  24.1 0.1 copy.106
  24.3 0.7 reshape.120
  25.0 0.2 slice.264
  25.2 0.1 fusion.44
  25.4 0.5 broadcast_compare_fusion
  25.9 0.5 broadcast_multiply_fusion.1
  26.3 25.2 %all_gather.7 = bf16[128,384]{0,1:T(8,128)(2,1)S(1)} all-gather(bf16[128,24]{0,1:T(8,128)(2,1)S(1)} %copy-done.3), channel_id=1, replica_groups=mesh['row'=8,'col'=16] {'col'}, dimensions={1}, use_global_device_ids=true | all-gather | bytes 104448 | tf_op jit(solution)/shard_map/all_gather | solution.py:146
  51.5 0.2 fusion.26
  51.8 0.7 copy-done.2
  52.4 0.6 slice.372
  53.1 0.1 mul.499
  53.2 0.2 copy.107
  53.3 0.8 copy.104
  54.1 0.8 copy.105
  54.9 0.6 slice_bitcast_fusion.9
  55.6 0.8 compare_convert_fusion
  56.3 0.7 reduce_sum.46
  57.0 1.6 fusion.47
  58.6 12.2 %fusion.38 = f32[12,128,512]{2,0,1:T(8,128)} fusion(bf16[128,512,128]{2,1,0:T(8,128)(2,1)} %param.31, bf16[128,12]{0,1:T(8,128)(2,1)} %param.38), kind=kOutput, calls=%fused_computation.69 | convolution fusion | flops 201326592 | bytes 19926016 | tf_op jit(solution)/shard_map/qkc,ch->hqk/dot_general | solution.py:79
  70.8 0.8 add_add_fusion
  71.6 0.8 add_add_fusion.2
  72.5 7.9 %fusion.45 = (f32[12,128]{1,0:T(8,128)S(1)}, f32[12,128,512]{2,1,0:T(8,128)}) fusion(bf16[3,12,4,512]{3,2,1,0:T(4,128)(2,1)} %reshape.120, f32[1,12,4,128]{3,2,0,1:T(4,128)S(1)} %bitcast.127, f32[1,12,4,128]{3,2,0,1:T(4,128)S(1)} %bitcast.131, f32[1,12,4,128]{3,2,0,1:T(4,128)S(1)} %bitcast.129, f32[12,512]{1,0:T(8,128)} %reduce_sum.46, ...), kind=kOutput, calls=%fused_computation.104 | convolution fusion | flops 122718720 | bytes 9957984 | tf_op jit(solution)/shard_map/ahpq,ahpk->hqk/dot_general | solution.py:80
  80.3 38.8 %pmax.7 = f32[12,128]{1,0:T(8,128)S(1)} all-reduce(f32[12,128]{1,0:T(8,128)S(1)} %get-tuple-element.46), channel_id=1, replica_groups=mesh['row'=8,'col'=16] {'col'}, use_global_device_ids=true, to_apply=%region_3.4 | all-reduce | flops 1536 | bytes 12288 | tf_op jit(solution)/shard_map/pmax | solution.py:179
  119.1 2.6 convert_reduce_fusion
  121.7 7.7 %fusion.10 = f32[12,128,128]{1,0,2:T(8,128)S(1)} fusion(bf16[128,512,128]{2,1,0:T(8,128)(2,1)} %param.31, bf16[12,128,512]{2,1,0:T(8,128)(2,1)S(1)} %get-tuple-element.8), kind=kOutput, calls=%fused_computation.14 | convolution fusion | flops 201326592 | bytes 19136512 | tf_op jit(solution)/shard_map/hqk,qkc->hcq/dot_general | solution.py:102
  129.4 0.5 fusion.13
  130.0 0.5 fusion.48
  130.5 0.3 copy.101
  130.9 0.9 fusion.16
  131.8 0.0 all-reduce.2.cloned.1.call-update
  131.9 35.5 %psum.29 = bf16[12,128]{1,0:T(8,128)(2,1)S(1)} all-reduce(bf16[12,128]{1,0:T(8,128)(2,1)S(1)} %get-tuple-element.5), channel_id=1, replica_groups=mesh['row'=8,'col'=16] {'col'}, use_global_device_ids=true, to_apply=%region_6.7 | all-reduce | flops 1536 | bytes 6144 | tf_op jit(solution)/shard_map/psum | solution.py:182
  167.4 45.8 %all-reduce.2.cloned.1.call-done = bf16[12,168,128]{2,1,0:T(8,128)(2,1)} async-done(((bf16[12,168,128]{2,1,0:T(8,128)(2,1)}), bf16[12,168,128]{2,1,0:T(8,128)(2,1)}) %all-reduce.2.cloned.1.call-update) | async-done | bytes 516112 | tf_op jit(solution)/shard_map/psum | solution.py:183
  213.2 1.2 convert_divide_fusion
  214.7 0.2 fusion.46
  214.9 38.2 %psum.30 = f32[128]{0:T(128)S(1)} all-reduce(f32[128]{0:T(128)S(1)} %get-tuple-element.48), channel_id=1, replica_groups=mesh['row'=8,'col'=16] {'col'}, use_global_device_ids=true, to_apply=%region_8.9 | all-reduce | flops 128 | bytes 1024 | tf_op jit(solution)/shard_map/psum | solution.py:189
  253.1 35.5 %psum.31 = f32[128]{0:T(128)S(1)} all-reduce(f32[128]{0:T(128)S(1)} %multiply_reduce_fusion.1), channel_id=1, replica_groups=mesh['row'=8,'col'=16] {'col'}, use_global_device_ids=true, to_apply=%region_10.11 | all-reduce | flops 128 | bytes 1024 | tf_op jit(solution)/shard_map/psum | solution.py:191
  288.6 0.7 add_convert_fusion.9
  (70 shorter events, 0.5 us)
Async XLA Ops:
  6.5 208.1 %copy-start = (bf16[2016,24]{0,1:T(8,128)(2,1)S(1)}, bf16[2016,24]{0,1:T(8,128)(2,1)}, u32[]{:S(2)}) copy-start(bf16[2016,24]{0,1:T(8,128)(2,1)} %param.41) | copy-start | bytes 290308
  6.5 206.6 %all-reduce.2.cloned.1.call-start = ((), (), s32[]{:S(2)}) async-start(), calls=%async_computation | async-start | bytes 1032192 | tf_op jit(solution)/shard_map/psum | solution.py:183
  9.0 16.4 %copy-start.19 = (s32[512]{0:T(512)S(1)}, s32[512]{0:T(512)}, u32[]{:S(2)}) copy-start(s32[512]{0:T(512)} %param.30) | copy-start | bytes 6148
  9.0 16.9 %copy-start.25 = (f32[12]{0:T(128)S(1)}, f32[12]{0:T(128)}, u32[]{:S(2)}) copy-start(f32[12]{0:T(128)} %param.39) | copy-start | bytes 148
  9.0 17.3 %copy-start.3 = (bf16[128,24]{0,1:T(8,128)(2,1)S(1)}, bf16[128,24]{0,1:T(8,128)(2,1)}, u32[]{:S(2)}) copy-start(bf16[128,24]{0,1:T(8,128)(2,1)} %param.22) | copy-start | bytes 18436
  9.0 42.5 %copy-start.23 = (bf16[384,192]{0,1:T(8,128)(2,1)S(1)}, bf16[384,192]{0,1:T(8,128)(2,1)}, u32[]{:S(2)}) copy-start(bf16[384,192]{0,1:T(8,128)(2,1)} %param.32) | copy-start | bytes 442372
  9.0 42.5 %copy-start.24 = (bf16[384,144]{0,1:T(8,128)(2,1)S(1)}, bf16[384,144]{0,1:T(8,128)(2,1)}, u32[]{:S(2)}) copy-start(bf16[384,144]{0,1:T(8,128)(2,1)} %param.33) | copy-start | bytes 331780
  24.1 30.8 %copy-start.4 = (f32[3,128]{1,0:T(4,128)S(1)}, f32[3,128]{1,0:T(4,128)}, u32[]{:S(2)}) copy-start(f32[3,128]{1,0:T(4,128)} %param.24) | copy-start | bytes 4612
  24.1 30.8 %copy-start.17 = (f32[9,128]{1,0:T(8,128)S(1)}, f32[9,128]{1,0:T(8,128)}, u32[]{:S(2)}) copy-start(f32[9,128]{1,0:T(8,128)} %param.23) | copy-start | bytes 13828
  24.1 31.4 %copy-start.18 = (s32[512]{0:T(512)S(1)}, s32[512]{0:T(512)}, u32[]{:S(2)}) copy-start(s32[512]{0:T(512)} %param.29) | copy-start | bytes 6148
  24.1 31.4 %copy-start.20 = (s32[128]{0:T(128)S(1)}, s32[128]{0:T(128)}, u32[]{:S(2)}) copy-start(s32[128]{0:T(128)} %param.25) | copy-start | bytes 1540
  51.8 0.7 copy-start.2
  55.5 15.3 %copy-start.6 = (f32[128]{0:T(128)}, f32[128]{0:T(128)S(1)}, u32[]{:S(2)}) copy-start(f32[128]{0:T(128)S(1)} %get-tuple-element.59) | copy-start | bytes 1540
  55.5 15.3 %copy-start.8 = (f32[128]{0:T(128)}, f32[128]{0:T(128)S(1)}, u32[]{:S(2)}) copy-start(f32[128]{0:T(128)S(1)} %get-tuple-element.60) | copy-start | bytes 1540
  121.7 8.2 %copy-start.1 = (bf16[192,512]{1,0:T(8,128)(2,1)S(1)}, bf16[192,512]{1,0:T(8,128)(2,1)}, u32[]{:S(2)}) copy-start(bf16[192,512]{1,0:T(8,128)(2,1)} %copy.104) | copy-start | bytes 589828
  130.5 83.9 %copy-start.5 = (f32[3,128]{1,0:T(4,128)S(1)}, f32[3,128]{1,0:T(4,128)}, u32[]{:S(2)}) copy-start(f32[3,128]{1,0:T(4,128)} %param.24) | copy-start | bytes 4612
  130.8 83.6 %copy-start.7 = (f32[128]{0:T(128)S(1)}, f32[128]{0:T(128)}, u32[]{:S(2)}) copy-start(f32[128]{0:T(128)} %copy-done.6) | copy-start | bytes 1540
  130.9 83.6 %copy-start.9 = (f32[128]{0:T(128)S(1)}, f32[128]{0:T(128)}, u32[]{:S(2)}) copy-start(f32[128]{0:T(128)} %copy-done.8) | copy-start | bytes 1540
  130.9 83.6 %copy-start.10 = (f32[128]{0:T(128)S(1)}, f32[128]{0:T(128)}, u32[]{:S(2)}) copy-start(f32[128]{0:T(128)} %get-tuple-element.61) | copy-start | bytes 1540
  130.9 83.6 %copy-start.11 = (f32[128]{0:T(128)S(1)}, f32[128]{0:T(128)}, u32[]{:S(2)}) copy-start(f32[128]{0:T(128)} %get-tuple-element.62) | copy-start | bytes 1540
  130.9 83.6 %copy-start.12 = (f32[128]{0:T(128)S(1)}, f32[128]{0:T(128)}, u32[]{:S(2)}) copy-start(f32[128]{0:T(128)} %get-tuple-element.63) | copy-start | bytes 1540
  130.9 83.6 %copy-start.13 = (f32[128]{0:T(128)S(1)}, f32[128]{0:T(128)}, u32[]{:S(2)}) copy-start(f32[128]{0:T(128)} %get-tuple-element.64) | copy-start | bytes 1540
  130.9 83.6 %copy-start.14 = (f32[128]{0:T(128)S(1)}, f32[128]{0:T(128)}, u32[]{:S(2)}) copy-start(f32[128]{0:T(128)} %get-tuple-element.65) | copy-start | bytes 1540
  130.9 83.6 %copy-start.15 = (f32[128]{0:T(128)S(1)}, f32[128]{0:T(128)}, u32[]{:S(2)}) copy-start(f32[128]{0:T(128)} %get-tuple-element.66) | copy-start | bytes 1540
  130.9 83.6 %copy-start.16 = (f32[128]{0:T(128)S(1)}, f32[128]{0:T(128)}, u32[]{:S(2)}) copy-start(f32[128]{0:T(128)} %get-tuple-element.67) | copy-start | bytes 1540
  131.8 156.8 %copy-start.21 = (f32[24]{0:T(128)S(1)}, f32[24]{0:T(128)}, u32[]{:S(2)}) copy-start(f32[24]{0:T(128)} %param.43) | copy-start | bytes 292
  131.8 156.8 %copy-start.22 = (f32[24]{0:T(128)S(1)}, f32[24]{0:T(128)}, u32[]{:S(2)}) copy-start(f32[24]{0:T(128)} %param.42) | copy-start | bytes 292
Sparse Core Ops, SparseCore 0:
  132.0 81.1 all-reduce.1
where the time goes:
time: 297 us; the launch traced here: 296 us
  blocking collectives  187 us (63%)
  waiting for transfers between devices  45.8 us (15%)
  matrix products  32.3 us (11%)
  between operations  13.9 us (5%)
  other arithmetic  10.3 us (3%)
  local copies, waits for them, and re-layouts  6.7 us (2%)
    psum x1, waiting for transfers between devices, on_device(): lax.psum((numerators * factor[:, None, :]).astype(jnp.bfloat16), 'col')  45.8 us
    pmax x1, blocking collectives, on_device(): highest = lax.pmax(maximum, 'col')  38.8 us
    psum x1, blocking collectives, on_device(): average = lax.psum(jnp.sum(mixed, axis=1), 'col') / D  38.2 us
    psum x1, blocking collectives, on_device(): lax.psum((weight_sum * factor).astype(jnp.bfloat16), 'col')  35.5 us
    psum x1, blocking collectives, on_device(): variance = lax.psum(jnp.sum(centred * centred, axis=1), 'col') / D  35.5 us
    all_gather x1, blocking collectives, on_device(): full_rows = lax.all_gather(query_single, 'col', axis=1, tiled=True)  25.2 us
    all_gather x1, blocking collectives, on_device(): package = lax.all_gather(own_rows, 'row', axis=1, tiled=True)  14 us
    dot_general x1, matrix products, block_partials(): jnp.einsum('qkc,ch->hqk', pair, pair_weight, preferred_element_type=jnp.f...  12.2 us
  transfers between devices with their start and end apart: 1, of which 1 were waited for; matrix products, arithmetic and copies ran while one was open for 0% of the time, Pallas kernels for 0%

commit v1 on v0

v1 whole, which is shorter than its diff:
```python
import jax
import jax.numpy as jnp
import numpy as np
from jax import lax
from jax.experimental import pallas as pl
from jax.experimental.pallas import tpu as pltpu
from jax.sharding import PartitionSpec as P

D = 384
H = 12
C = 16
PQ = 4
PV = 8
CZ = 128
FEAT = 168
QB = 8
RB = QB * H

LOGIT_SCALE = (1.0 / 3.0) ** 0.5
POINT_SCALE = (2.0 / (9.0 * PQ)) ** 0.5 * 0.5
NORM_EPS = 1e-05
MASKED = -1000000000.0
PRECISE = lax.Precision.HIGHEST
F32 = jnp.float32
BF16 = jnp.bfloat16

CHAIN_AT = H * C
POINTS_AT = CHAIN_AT + 3 * 16
NORMS_AT = POINTS_AT + 3 * 3 * H * PQ
DEPTH = NORMS_AT + 6 * 16
SUM_AT = H * C + 3 * H * PV
WIDE = 512
CHUNK = RB + 48


def head_masks():
    head = (np.arange(RB) % H)[:, None]
    k = np.arange(DEPTH)[None, :]
    of_k = np.where(
        k < CHAIN_AT,
        k // C,
        np.where(
            k < POINTS_AT,
            -1,
            np.where(k < NORMS_AT, ((k - POINTS_AT) % (H * PQ)) // PQ, (k - NORMS_AT) % 16),
        ),
    )
    f = np.arange(WIDE)[None, :]
    of_f = np.where(
        f < H * C,
        f // C,
        np.where(f < SUM_AT, ((f - H * C) % (H * PV)) // PV, f - SUM_AT),
    )
    lane = np.arange(128)[None, :]
    spread = (np.arange(128)[:, None] == of_f) & (f < SUM_AT)
    return (
        (head == of_k).astype(np.float32),
        (head == of_f).astype(np.float32),
        (head == lane).astype(np.float32),
        spread.astype(np.float32),
    )


def split(x):
    first = x.astype(BF16)
    rest = x - first.astype(F32)
    second = rest.astype(BF16)
    third = (rest - second.astype(F32)).astype(BF16)
    return first, second, third


def dot(a, b, ca=1, cb=0, precision=None):
    return lax.dot_general(
        a, b, (((ca,), (cb,)), ((), ())), precision=precision, preferred_element_type=F32
    )


def iota(shape, axis):
    return lax.broadcasted_iota(jnp.int32, shape, axis)


def row_of(rows, first):
    gap = iota((rows, 128), 0) - H * (iota((rows, 128), 1) - first)
    return jnp.where((gap >= 0) & (gap < H), 1.0, 0.0).astype(BF16)


def pack_kernel(cols, rows, qs, ks, krot, kanc, ow, q_out, k_out, w_out):
    turned = qs[...].astype(F32).T.astype(BF16)
    for c in range(cols):
        q_out[c] = turned
    frames = jnp.concatenate([krot[...], kanc[...], jnp.zeros((4, krot.shape[1]), F32)], axis=0)
    parts = jnp.concatenate([p.astype(F32) for p in split(frames)], axis=0)
    frames = jnp.concatenate([parts, jnp.zeros((80, krot.shape[1]), F32)], axis=0).T.astype(BF16)
    for r in range(rows):
        k_out[r, :, :D] = ks[...]
        k_out[r, :, D:] = frames
    w = ow[...].astype(F32)
    pieces = [w[h * FEAT + 40 : (h + 1) * FEAT] for h in range(H)]
    pieces += [w[h * FEAT : h * FEAT + C] for h in range(H)]
    for a in range(3):
        start = C + a * PV
        pieces += [w[h * FEAT + start : h * FEAT + start + PV] for h in range(H)]
    w = jnp.concatenate(pieces, axis=0).astype(BF16)
    width = w.shape[1]
    eye = jnp.where(iota((width, width), 0) == iota((width, width), 1), 1.0, 0.0).astype(BF16)
    w_out[...] = dot(eye, w, 1, 1).astype(BF16)


def bias_kernel(pair, pw, out):
    gap = iota((2 * H, H), 0) - iota((2 * H, H), 1)
    pick = jnp.where((gap == 0) | (gap == H), 1.0, 0.0).astype(BF16)
    turned = dot(pick, pw[...], 1, 1)
    row = iota((2 * H, CZ), 0)
    weights = jnp.concatenate(
        [jnp.where(row < H, turned, 0.0), jnp.where(row < H, 0.0, turned)], axis=1
    ).astype(BF16)
    for p in range(QB // 2):
        both = jnp.concatenate([pair[2 * p], pair[2 * p + 1]], axis=1)
        out[2 * H * p : 2 * H * (p + 1)] = dot(weights, both, 1, 1)


def rotated(rot, anc, local):
    size = local.shape[0] // 3
    part = [local[size * b : size * (b + 1)] for b in range(3)]
    return [
        rot[3 * a : 3 * a + 1] * part[0]
        + rot[3 * a + 1 : 3 * a + 2] * part[1]
        + rot[3 * a + 2 : 3 * a + 3] * part[2]
        + anc[a : a + 1]
        for a in range(3)
    ]


def attend_kernel(
    blocks,
    qall,
    qrot,
    qanc,
    qchain,
    kall,
    kchain,
    kmask,
    qw,
    qpw,
    kw,
    vw,
    kpw,
    vpw,
    gamma,
    gap,
    mask_k,
    mask_f,
    mask_h,
    bias,
    pair_hbm,
    out,
    pair,
    left,
    logits,
    attn,
    extra,
    sems,
):
    def fetch(b):
        return pltpu.make_async_copy(
            pair_hbm.at[pl.ds(QB * b, QB)], pair.at[pl.ds(QB * b, QB)], sems.at[b]
        )

    for b in range(blocks):
        fetch(b).start()

    scale = gamma[...] * POINT_SCALE
    by_point = jnp.where((iota((H * PQ, H), 0) >> 2) == iota((H * PQ, H), 1), scale, 0.0)
    by_point = jnp.sum(by_point, axis=1, keepdims=True)
    by_head = jnp.where(iota((16, H), 0) == iota((16, H), 1), scale, 0.0)
    by_head = jnp.sum(by_head, axis=1, keepdims=True)
    heads = jnp.where(iota((16, H * PQ), 0) == (iota((16, H * PQ), 1) >> 2), 1.0, 0.0)

    def norms(points):
        squares = points[0] * points[0] + points[1] * points[1] + points[2] * points[2]
        return split(-by_head * dot(heads, squares, precision=PRECISE))

    q = dot(qw[...], qall[...], 0, 0).astype(BF16).astype(F32) * C ** (-0.5)
    points = rotated(qrot[...], qanc[...], dot(qpw[...], qall[...], 0, 0))
    first, second, third = split(jnp.concatenate([2.0 * by_point * p for p in points], axis=0))
    count = qall.shape[1]
    chain = jnp.where(iota((16, count), 0) == qchain[...], 1.0, 0.0).astype(BF16)
    ones = jnp.ones((16, count), BF16)
    table = jnp.concatenate(
        [q.astype(BF16), chain, chain, chain, first, second, third, *norms(points), ones, ones, ones],
        axis=0,
    )

    rows = kall[:, :D]
    keys = kall.shape[0]
    eye = jnp.where(iota((128, 128), 0) == iota((128, 128), 1), 1.0, 0.0).astype(BF16)
    frames = dot(eye, kall[:, D:], 1, 1)
    frames = (frames[0:16] + frames[16:32]) + frames[32:48]
    krot, kanc = frames[0:9], frames[9:12]

    def project(weight):
        return dot(weight[...], rows, 0, 1)

    kpoints = [p.astype(BF16) for p in rotated(krot, kanc, project(kpw))]
    vpoints = [p.astype(BF16) for p in rotated(krot, kanc, project(vpw))]
    apart = jnp.where(iota((16, keys), 0) != kchain[...], 1.0, 0.0).astype(BF16)
    kones = jnp.ones((16, keys), BF16)
    right = jnp.concatenate(
        [
            project(kw).astype(BF16),
            apart,
            apart,
            apart,
            *kpoints,
            *kpoints,
            *kpoints,
            kones,
            kones,
            kones,
            *norms([p.astype(F32) for p in kpoints]),
        ],
        axis=0,
    )
    values = jnp.concatenate(
        [project(vw).astype(BF16), *vpoints, kones, jnp.zeros((16, keys), BF16)], axis=0
    )

    head_lane = mask_h[...]
    own_gap = jnp.sum(head_lane[:, :H] * gap[...], axis=1, keepdims=True)
    lane = iota((RB, DEPTH), 1)
    by_column = mask_k[...]
    for t, part in enumerate(split(own_gap)):
        inside = (lane >= CHAIN_AT + 16 * t) & (lane < CHAIN_AT + 16 * (t + 1))
        by_column = jnp.where(inside, part.astype(F32), by_column)
    for b in range(blocks):
        left[RB * b : RB * (b + 1)] = (dot(row_of(RB, QB * b), table, 1, 1) * by_column).astype(BF16)
    tall = 4 * RB
    for g in range(blocks // 4):
        logits[tall * g : tall * (g + 1)] = dot(left[tall * g : tall * (g + 1)], right)

    real = kmask[...] > 0
    lanes = [head_lane] + [pltpu.roll(head_lane, 16 * t, 1) for t in range(1, 4)]
    for b in range(blocks):
        at = slice(RB * b, RB * (b + 1))
        x = jnp.where(real, LOGIT_SCALE * (logits[at] + bias[at]), MASKED)
        top = jnp.max(x, axis=1, keepdims=True)
        e = jnp.exp(x - top)
        attn[at] = e.astype(BF16)
        tops = [p.astype(F32) for p in split(top)]
        extra[at] = tops[0] * lanes[0] + tops[1] * lanes[1] + tops[2] * lanes[2]
        fetch(b).wait()
        upper = iota((2 * H, CZ), 0) < H
        for p in range(QB // 2):
            i = QB * b + 2 * p
            both = jnp.concatenate([pair[i], pair[i + 1]], axis=1)
            z = dot(e[2 * H * p : 2 * H * (p + 1)].astype(BF16), both)
            z = jnp.where(upper, z[:, :CZ], z[:, CZ:])
            logits[RB * b + 2 * H * p : RB * b + 2 * H * (p + 1), :CZ] = z
        out[b, :RB] = logits[at, :CZ].astype(BF16)

    by_lane = mask_f[...]
    own = iota((QB, RB), 1) - H * iota((QB, RB), 0)
    own = jnp.where((own >= 0) & (own < H), 1.0, 0.0).astype(BF16)
    for g in range(blocks // 4):
        wide = dot(attn[tall * g : tall * (g + 1)], values, 1, 1)
        for s in range(4):
            b = 4 * g + s
            mine = wide[RB * s : RB * (s + 1)] * by_lane
            rounded = mine.astype(BF16)
            last = mine[:, 384:] - rounded[:, 384:].astype(F32)
            rest = extra[RB * b : RB * (b + 1)] + pltpu.roll(last, 80, 1) * lanes[3]
            packed = dot(own, rounded)
            tail = dot(own, rest.astype(BF16))
            out[b, RB:] = jnp.concatenate(
                [packed[:, 128 * t : 128 * (t + 1)] for t in range(4)]
                + [tail, jnp.zeros((8, 128), F32)],
                axis=0,
            ).astype(BF16)


def finish_kernel(cols, got, qall, qrot, qanc, weights, mask_h, spread, out, rows):
    tail = got[:, RB:, :].astype(F32)
    count = cols * QB

    def tile(t):
        return tail[:, QB * t : QB * (t + 1)].reshape(count, 128)

    marks = tile(4)
    top = (marks + pltpu.roll(marks, 112, 1)) + pltpu.roll(marks, 96, 1)
    sums = pltpu.roll(tile(3), 32, 1) + pltpu.roll(marks, 80, 1)
    top = top.reshape(cols, QB, 128)
    factor = jnp.exp(top - jnp.max(top, axis=0, keepdims=True))
    total = jnp.sum(sums.reshape(cols, QB, 128) * factor, axis=0, keepdims=True)
    head = iota((cols, QB, 128), 2) < H
    factor = jnp.where(head, factor / total, 0.0).reshape(count, 128)
    high, low, _ = split(factor)
    wide = dot(high, spread[...]) + dot(low, spread[...])
    averaged = [
        jnp.sum((tile(t) * wide[:, 128 * t : 128 * (t + 1)]).reshape(cols, QB, 128), axis=0)
        for t in range(4)
    ]
    averaged = jnp.concatenate(averaged, axis=1)

    z = jnp.zeros((RB, CZ), F32)
    for c in range(cols):
        pick = row_of(RB, QB * c)
        mine = (dot(pick, high) + dot(pick, low)) * mask_h[...]
        z = z + got[c, :RB].astype(F32) * jnp.sum(mine, axis=1, keepdims=True)
    rows[...] = z

    me = lax.axis_index("col")
    own = iota((QB, 128), 1) == QB * me + iota((QB, 128), 0)

    def mine(ref, k):
        return jnp.sum(jnp.where(own, ref[k : k + 1], 0.0), axis=1, keepdims=True)

    cut = H * C
    step = H * PV
    shifted = [averaged[:, cut + step * b : cut + step * (b + 1)] - mine(qanc, b) for b in range(3)]
    local = [
        mine(qrot, a) * shifted[0] + mine(qrot, 3 + a) * shifted[1] + mine(qrot, 6 + a) * shifted[2]
        for a in range(3)
    ]
    features = [rows[pl.ds(h, QB, stride=H), :] for h in range(H)] + [averaged[:, :cut]] + local
    features = jnp.concatenate(features, axis=1).astype(BF16)
    mixed = dot(jnp.where(own, 1.0, 0.0).astype(BF16), qall[...], 1, 1)
    mixed = mixed + dot(features, weights[...], 1, 1)
    centred = mixed - jnp.sum(mixed, axis=1, keepdims=True) * (1.0 / D)
    variance = jnp.sum(centred * centred, axis=1, keepdims=True) * (1.0 / D)
    normal = centred * lax.rsqrt(variance + NORM_EPS)
    width = D // cols
    for c in range(cols):
        out[c] = normal[:, width * c : width * (c + 1)]


def call(kernel, out_shape, scratch=(), **params):
    return pl.pallas_call(
        kernel,
        out_shape=out_shape,
        scratch_shapes=scratch,
        compiler_params=pltpu.CompilerParams(vmem_limit_bytes=48 << 20, **params),
    )


def shape(dims, dtype):
    return jax.ShapeDtypeStruct(dims, dtype)


def on_device(
    query_single,
    query_rotation,
    query_anchor,
    query_chain,
    key_single,
    key_rotation,
    key_anchor,
    key_chain,
    key_mask,
    pair_tile,
    query_weight,
    query_point_weight,
    key_weight,
    value_weight,
    key_point_weight,
    value_point_weight,
    pair_weight,
    head_gamma,
    chain_gap,
    out_weight,
    norm_gain,
    norm_shift,
):
    rows, cols = lax.axis_size("row"), lax.axis_size("col")
    queries, width = query_single.shape
    own_keys = key_single.shape[0]
    keys = rows * own_keys
    blocks = queries // QB
    mask_k, mask_f, mask_h, spread = (jnp.asarray(m) for m in head_masks())

    def send(x, axis):
        return lax.all_to_all(x, axis, 0, 0)

    q_pack, k_pack, w_pack = call(
        lambda *refs: pack_kernel(cols, rows, *refs),
        (
            shape((cols, width, queries), BF16),
            shape((rows, own_keys, 512), BF16),
            shape((width, H * FEAT), BF16),
        ),
    )(query_single, key_single, key_rotation, key_anchor, out_weight)
    qall = send(q_pack, "col").reshape(D, queries)
    kall = send(k_pack, "row").reshape(keys, 512)
    weights = lax.all_gather(w_pack, "col", axis=0, tiled=True)

    bias = pl.pallas_call(
        bias_kernel,
        grid=(blocks,),
        in_specs=[
            pl.BlockSpec((QB, keys, CZ), lambda b: (b, 0, 0)),
            pl.BlockSpec((CZ, H), lambda b: (0, 0)),
        ],
        out_specs=pl.BlockSpec((RB, keys), lambda b: (b, 0)),
        out_shape=shape((blocks * RB, keys), F32),
        compiler_params=pltpu.CompilerParams(vmem_limit_bytes=32 << 20),
        cost_estimate=pl.CostEstimate(
            flops=2 * queries * keys * CZ * 128,
            bytes_accessed=queries * keys * CZ * 2,
            transcendentals=0,
        ),
    )(pair_tile, pair_weight)

    whole = pl.BlockSpec(memory_space=pltpu.VMEM)
    parts = pl.pallas_call(
        lambda *refs: attend_kernel(blocks, *refs),
        in_specs=[whole] * 19 + [pl.BlockSpec(memory_space=pl.ANY)],
        out_specs=whole,
        out_shape=shape((blocks, CHUNK, 128), BF16),
        scratch_shapes=[
            pltpu.VMEM((queries, keys, CZ), BF16),
            pltpu.VMEM((blocks * RB, DEPTH), BF16),
            pltpu.VMEM((blocks * RB, keys), F32),
            pltpu.VMEM((blocks * RB, keys), BF16),
            pltpu.VMEM((blocks * RB, 128), F32),
            pltpu.SemaphoreType.DMA((blocks,)),
        ],
        compiler_params=pltpu.CompilerParams(vmem_limit_bytes=48 << 20),
    )(
        qall,
        query_rotation,
        query_anchor,
        query_chain.reshape(1, -1),
        kall,
        key_chain.reshape(1, -1),
        key_mask.reshape(1, -1),
        query_weight,
        query_point_weight,
        key_weight,
        value_weight,
        key_point_weight,
        value_point_weight,
        head_gamma.reshape(1, -1),
        chain_gap.reshape(1, -1),
        mask_k,
        mask_f,
        mask_h,
        bias,
        pair_tile,
    )
    got = send(parts, "col")
    normal = call(
        lambda *refs: finish_kernel(cols, *refs),
        shape((cols, QB, width), F32),
        [pltpu.VMEM((RB, CZ), F32)],
    )(got, qall, query_rotation, query_anchor, weights, mask_h, spread.astype(BF16))
    normal = send(normal, "col").reshape(queries, width)
    return (normal * norm_gain + norm_shift).astype(BF16)


def solution(mesh):
    placed = (
        P("row", "col"),
        P(None, "row"),
        P(None, "row"),
        P("row"),
        P(("col", "row"), None),
        P(None, ("col", "row")),
        P(None, ("col", "row")),
        P("col"),
        P("col"),
        P("row", "col", None),
        P(),
        P(),
        P(),
        P(),
        P(),
        P(),
        P(),
        P(),
        P(),
        P(None, "col"),
        P("col"),
        P("col"),
    )
    return jax.shard_map(
        on_device, mesh=mesh, in_specs=placed, out_specs=P("row", "col"), check_vma=False
    )
```

time: 297 us -> 116 us (0.39)
  blocking collectives: 187 us -> 42.7 us
  waiting for transfers between devices: 45.8 us -> 0.02 us
  matrix products: 32.3 us -> 0 us
  local copies, waits for them, and re-layouts: 6.7 us -> 31.3 us
  Pallas kernels: 0 us -> 21.9 us
  other arithmetic: 10.3 us -> 1.38 us
  starting transfers between devices: 0.01 us -> 4.31 us
    psum x3 -> x0, blocking collectives: 109 us -> none  [the longest x1 38.2 us: on_device(): average = lax.psum(jnp.sum(mixed, axis=1), 'col') / D]
    psum x1 -> x0, waiting for transfers between devices: 45.8 us -> none  [on_device(): lax.psum((numerators * factor[:, None, :]).astype(jnp.bfloat16), 'col')]
    all_to_all x0 -> x3, blocking collectives: none -> 42.7 us  [send(): return lax.all_to_all(x, axis, 0, 0)]
    all_gather x2 -> x0, blocking collectives: 39.1 us -> none  [the longest x1 25.2 us: on_device(): full_rows = lax.all_gather(query_single, 'col', axis=1, tiled=True)]
    pmax x1 -> x0, blocking collectives: 38.8 us -> none  [on_device(): highest = lax.pmax(maximum, 'col')]
    dot_general x9 -> x0, matrix products: 32.3 us -> none  [the longest x1 12.2 us: block_partials(): jnp.einsum('qkc,ch->hqk', pair, pair_weight, preferred_element_type=jnp.f...]
    unnamed x56 -> x71, local copies, waits for them, and re-layouts: 2.62 us -> 30.8 us
    pallas_call x0 -> x4, Pallas kernels: none -> 21.9 us  [the longest x1 11.5 us: on_device(): pl.pallas_call(lambda *refs: attend_kernel(blocks, *refs), in_specs=[whol...]
  transfers between devices with their start and end apart: 1 -> 2, of which waited for: 1 -> 0; matrix products, arithmetic and copies ran while one was open for 0% -> 6% of each run, Pallas kernels for 0% -> 17%
where the time goes in v1:
time: 116 us; the launch traced here: 115 us
  blocking collectives  42.7 us (37%)
  local copies, waits for them, and re-layouts  31.3 us (27%)
  Pallas kernels  21.9 us (19%)
  between operations  13.5 us (12%)
  starting transfers between devices  4.31 us (4%)
  other arithmetic  1.38 us (1%)
    all_to_all x3, blocking collectives, send(): return lax.all_to_all(x, axis, 0, 0)  42.7 us
    unnamed x71, local copies, waits for them, and re-layouts  30.8 us
    pallas_call x1, Pallas kernels, on_device(): pl.pallas_call(lambda *refs: attend_kernel(blocks, *refs), in_specs=[whol...  11.5 us
    pallas_call x1, Pallas kernels, on_device(): pl.pallas_call(bias_kernel, grid=(blocks,), in_specs=[pl.BlockSpec((QB, k...  7.92 us
    all_to_all x1, starting transfers between devices, send(): return lax.all_to_all(x, axis, 0, 0)  4.28 us
  transfers between devices with their start and end apart: 2, of which 0 were waited for; matrix products, arithmetic and copies ran while one was open for 6% of the time, Pallas kernels for 17%

profile of v1, /device:TPU:0, one launch (start us, length us, event | category | flops | bytes accessed | tf_op | source)
XLA Modules:
  0.0 115.2 jit_solution(15979900001952856357)
XLA Ops:
  6.5 0.0 all-gather.2.cloned.1.call-start
  6.6 1.3 %copy.28.refs_4_ = bf16[2016,24]{1,0:T(8,128)(2,1)S(1)} copy(bf16[2016,24]{0,1:T(8,128)(2,1)} %param.45) | data formatting | bytes 193536 | tf_op args[19]
  7.8 0.8 copy.27.refs_0_
  8.7 0.8 copy-done.13
  9.5 0.7 copy-done.15
  10.2 0.7 copy-done.17
  10.8 1.1 shard_map.244
  11.9 0.0 all-gather.2.cloned.1.call-update
  12.0 15.7 %all_to_all.20 = bf16[16,24,128]{2,1,0:T(8,128)(2,1)S(1)} all-to-all(bf16[16,24,128]{2,1,0:T(8,128)(2,1)S(1)} %get-tuple-element.8), channel_id=1, replica_groups=mesh['row'=8,'col'=16] {'col'}, dimensions={0} | all-to-all | bytes 196608 | tf_op jit(solution)/shard_map/all_to_all | solution.py:381
  27.7 4.3 %all-to-all-start.1 = ((bf16[8,64,512]{2,1,0:T(8,128)(2,1)}), bf16[8,64,512]{2,1,0:T(8,128)(2,1)}, u32[]{:S(2)}, u32[]{:S(2)}) async-start(bf16[8,64,512]{2,1,0:T(8,128)(2,1)} %get-tuple-element.9), calls=%async_computation.1 | async-start | bytes 1048576 | tf_op jit(solution)/shard_map/all_to_all | solution.py:381
  31.9 1.4 %copy.29.pw = bf16[128,12]{1,0:T(8,128)(2,1)} copy(bf16[128,12]{0,1:T(8,128)(2,1)} %param.42) | data formatting | bytes 6144 | tf_op args[16]
  33.3 1.1 copy.35.refs_12_
  34.5 0.8 copy.30.refs_7_
  35.3 0.8 copy.31.refs_8_
  36.1 0.8 copy.32.refs_9_
  37.0 0.8 copy.33.refs_10_
  37.8 0.8 copy.34.refs_11_
  38.6 5.8 %copy-done = bf16[128,512,128]{2,1,0:T(8,128)(2,1)S(1)} copy-done((bf16[128,512,128]{2,1,0:T(8,128)(2,1)S(1)}, bf16[128,512,128]{2,1,0:T(8,128)(2,1)}, u32[]{:S(2)}) %copy-start) | copy-done | bytes 16777240
  44.4 0.8 copy-done.11
  45.2 7.9 %shard_map.245.refs_18_ = f32[1536,512]{1,0:T(8,128)S(1)} custom-call(bf16[128,512,128]{2,1,0:T(8,128)(2,1)S(1)} %copy-done, bf16[128,12]{1,0:T(8,128)(2,1)S(1)} %copy-done.11), custom_call_target="tpu_custom_call" | custom-call | flops 2147483648 | bytes 16777216 | tf_op jit(solution)/shard_map/pallas_call | solution.py:395
  53.1 0.0 copy-done.14
  53.1 0.9 copy-done.2
  54.1 0.9 copy-done.3
  55.0 0.9 copy-done.4
  55.9 0.9 copy-done.5
  56.9 0.9 copy-done.6
  57.8 1.0 copy-done.7
  58.8 0.9 copy-done.8
  59.7 0.8 copy-done.9
  60.5 0.7 copy-done.19
  61.2 0.7 copy-done.20
  61.8 0.7 copy-done.21
  62.5 0.7 copy-done.22
  63.1 11.5 %shard_map.246 = bf16[16,144,128]{2,1,0:T(8,128)(2,1)S(1)} custom-call(bf16[384,128]{1,0:T(8,128)(2,1)S(1)} %bitcast.8, f32[9,128]{1,0:T(8,128)S(1)} %copy-done.14, f32[3,128]{1,0:T(4,128)S(1)} %copy-done.16, s32[1,128]{1,0:T(1,128)S(1)} %bitcast.12, bf16[512,512]{1,0:T(8,128)(2,1)} %bitcast.2.refs_4_, s32[1,512]{1,0:T(1,128)S(1)} %bitcast.10, ...), custom_call_target="tpu_custom_call" | custom-call | tf_op jit(solution)/shard_map/pallas_call | solution.py:413
  74.6 0.0 copy-start.28
  74.6 0.0 copy-start.29
  74.6 16.2 %all_to_all.21.refs_0_ = bf16[16,144,128]{2,1,0:T(8,128)(2,1)S(1)} all-to-all(bf16[16,144,128]{2,1,0:T(8,128)(2,1)S(1)} %shard_map.246), channel_id=1, replica_groups=mesh['row'=8,'col'=16] {'col'}, dimensions={0} | all-to-all | bytes 1179648 | tf_op jit(solution)/shard_map/all_to_all | solution.py:381
  90.9 1.4 %copy-done.1 = bf16[384,2016]{1,0:T(8,128)(2,1)S(1)} copy-done((bf16[384,2016]{1,0:T(8,128)(2,1)S(1)}, bf16[384,2016]{1,0:T(8,128)(2,1)}, u32[]{:S(2)}) %copy-start.1) | copy-done | bytes 1548312
  92.3 0.8 copy-done.10
  93.1 0.9 copy-done.12
  94.0 1.4 %shard_map.247 = f32[16,8,24]{2,1,0:T(8,128)S(1)} custom-call(bf16[16,144,128]{2,1,0:T(8,128)(2,1)S(1)} %all_to_all.21.refs_0_, bf16[384,128]{1,0:T(8,128)(2,1)S(1)} %bitcast.9, f32[9,128]{1,0:T(8,128)S(1)} %copy-done.14, f32[3,128]{1,0:T(4,128)S(1)} %copy-done.16, bf16[384,2016]{1,0:T(8,128)(2,1)S(1)} %copy-done.1, f32[96,128]{1,0:T(8,128)S(1)} %copy-done.10, ...), custom_call_target="tpu_custom_call" | custom-call | tf_op jit(solution)/shard_map/pallas_call | solution.py:450
  95.4 0.1 reshape.34
  95.5 10.8 %all_to_all.22 = f32[16,1,192]{2,1,0:T(1,128)S(1)} all-to-all(f32[16,1,192]{2,1,0:T(1,128)S(1)} %reshape.34), channel_id=1, replica_groups=mesh['row'=8,'col'=16] {'col'}, dimensions={0} | all-to-all | bytes 24576 | tf_op jit(solution)/shard_map/all_to_all | solution.py:381
  106.3 0.5 broadcast.2
  106.9 0.7 reduce
  107.5 0.1 reshape.35
  107.6 0.1 copy.36
  107.7 0.7 add_convert_fusion
  (39 shorter events, 0.1 us)
Async XLA Ops:
  6.5 28.0 %copy-start.23 = (bf16[384,192]{0,1:T(8,128)(2,1)S(1)}, bf16[384,192]{0,1:T(8,128)(2,1)}, u32[]{:S(2)}) copy-start(bf16[384,192]{0,1:T(8,128)(2,1)} %param.36) | copy-start | bytes 442372
  6.5 28.8 %copy-start.26 = (bf16[384,144]{0,1:T(8,128)(2,1)S(1)}, bf16[384,144]{0,1:T(8,128)(2,1)}, u32[]{:S(2)}) copy-start(bf16[384,144]{0,1:T(8,128)(2,1)} %param.37) | copy-start | bytes 331780
  6.5 29.6 %copy-start.24 = (bf16[384,192]{0,1:T(8,128)(2,1)S(1)}, bf16[384,192]{0,1:T(8,128)(2,1)}, u32[]{:S(2)}) copy-start(bf16[384,192]{0,1:T(8,128)(2,1)} %param.38) | copy-start | bytes 442372
  6.5 30.4 %copy-start.25 = (bf16[384,192]{0,1:T(8,128)(2,1)S(1)}, bf16[384,192]{0,1:T(8,128)(2,1)}, u32[]{:S(2)}) copy-start(bf16[384,192]{0,1:T(8,128)(2,1)} %param.39) | copy-start | bytes 442372
  6.5 84.3 %all-gather.2.cloned.1.call-start = ((), (), s32[]{:S(2)}) async-start(), calls=%async_computation.4 | async-start | bytes 1671168 | tf_op jit(solution)/shard_map/all_gather | solution.py:393
  8.7 0.8 copy-start.13
  9.5 0.7 copy-start.15
  10.2 0.7 copy-start.17
  10.8 27.0 %copy-start.27 = (bf16[384,144]{0,1:T(8,128)(2,1)S(1)}, bf16[384,144]{0,1:T(8,128)(2,1)}, u32[]{:S(2)}) copy-start(bf16[384,144]{0,1:T(8,128)(2,1)} %param.40) | copy-start | bytes 331780
  27.7 25.4 %all-to-all-start.1 = ((bf16[8,64,512]{2,1,0:T(8,128)(2,1)}), bf16[8,64,512]{2,1,0:T(8,128)(2,1)}, u32[]{:S(2)}, u32[]{:S(2)}) async-start(bf16[8,64,512]{2,1,0:T(8,128)(2,1)} %get-tuple-element.9), calls=%async_computation.1 | async-start | bytes 1048576 | tf_op jit(solution)/shard_map/all_to_all | solution.py:381
  38.6 5.8 %copy-start = (bf16[128,512,128]{2,1,0:T(8,128)(2,1)S(1)}, bf16[128,512,128]{2,1,0:T(8,128)(2,1)}, u32[]{:S(2)}) copy-start(bf16[128,512,128]{2,1,0:T(8,128)(2,1)} %refs_19_.1) | copy-start | bytes 50331652
  44.4 0.8 copy-start.11
  45.2 8.0 %copy-start.14 = (f32[9,128]{1,0:T(8,128)S(1)}, f32[9,128]{1,0:T(8,128)}, u32[]{:S(2)}) copy-start(f32[9,128]{1,0:T(8,128)} %refs_2_.5) | copy-start | bytes 13828
  45.2 8.0 %copy-start.16 = (f32[3,128]{1,0:T(4,128)S(1)}, f32[3,128]{1,0:T(4,128)}, u32[]{:S(2)}) copy-start(f32[3,128]{1,0:T(4,128)} %refs_3_.3) | copy-start | bytes 4612
  45.2 8.0 %copy-start.18 = (s32[512]{0:T(512)S(1)}, s32[512]{0:T(512)}, u32[]{:S(2)}) copy-start(s32[512]{0:T(512)} %param.33) | copy-start | bytes 6148
  53.1 0.9 copy-start.2
  54.1 0.9 copy-start.3
  55.0 0.9 copy-start.4
  55.9 0.9 copy-start.5
  56.9 0.9 copy-start.6
  57.8 1.0 copy-start.7
  58.7 0.9 copy-start.8
  59.7 0.8 copy-start.9
  60.5 0.7 copy-start.19
  61.2 0.7 copy-start.20
  61.8 0.7 copy-start.21
  62.5 0.7 copy-start.22
  74.6 33.1 %copy-start.28 = (f32[24]{0:T(128)S(1)}, f32[24]{0:T(128)}, u32[]{:S(2)}) copy-start(f32[24]{0:T(128)} %param.47) | copy-start | bytes 292
  74.6 33.1 %copy-start.29 = (f32[24]{0:T(128)S(1)}, f32[24]{0:T(128)}, u32[]{:S(2)}) copy-start(f32[24]{0:T(128)} %param.46) | copy-start | bytes 292
  90.9 1.4 %copy-start.1 = (bf16[384,2016]{1,0:T(8,128)(2,1)S(1)}, bf16[384,2016]{1,0:T(8,128)(2,1)}, u32[]{:S(2)}) copy-start(bf16[384,2016]{1,0:T(8,128)(2,1)} %all-gather.2.cloned.1.call-done.refs_4_) | copy-start | bytes 4644868
  92.3 0.8 copy-start.10
  93.1 0.9 copy-start.12
Sparse Core Ops, SparseCore 0:
  12.1 46.6 all-gather.1

commit v2 on v0

v2 whole, which is shorter than its diff:
```python
import jax
import jax.numpy as jnp
from jax import lax
from jax.experimental import pallas as pl
from jax.experimental.pallas import tpu as pltpu
from jax.sharding import PartitionSpec as P

D = 384
H = 12
C = 16
PQ = 4
PV = 8
CZ = 128
FEAT = 168
QB = 8
RB = QB * H

LOGIT_SCALE = (1.0 / 3.0) ** 0.5
POINT_SCALE = (2.0 / (9.0 * PQ)) ** 0.5 * 0.5
NORM_EPS = 1e-05
MASKED = -1000000000.0
PRECISE = lax.Precision.HIGHEST
F32 = jnp.float32
BF16 = jnp.bfloat16

CHAIN_AT = H * C
POINTS_AT = CHAIN_AT + 3 * 16
NORMS_AT = POINTS_AT + 3 * 3 * H * PQ
DEPTH = NORMS_AT + 6 * 16
SUM_AT = H * C + 3 * H * PV
WIDE = 512
VMEM_BYTES = 63_400_000
SMALL = 11
KEY_SMALL = 12
AHEAD = 8
TALL = 8
HALF = 1024
CHUNK = RB + 48


def split(x):
    first = x.astype(BF16)
    rest = x - first.astype(F32)
    second = rest.astype(BF16)
    third = (rest - second.astype(F32)).astype(BF16)
    return first, second, third


def dot(a, b, ca=1, cb=0, precision=None):
    return lax.dot_general(
        a, b, (((ca,), (cb,)), ((), ())), precision=precision, preferred_element_type=F32
    )


def iota(shape, axis):
    return lax.broadcasted_iota(jnp.int32, shape, axis)


def head_row(shape_):
    row = iota(shape_, 0)
    return row - H * ((row * 43) >> 9)


def column_heads():
    k = iota((RB, DEPTH), 1)
    point = k - POINTS_AT
    for _ in range(8):
        point = jnp.where(point >= H * PQ, point - H * PQ, point)
    of_chain = jnp.where(k < POINTS_AT, -1, point >> 2)
    return jnp.where(k < CHAIN_AT, k >> 4, jnp.where(k < NORMS_AT, of_chain, (k - NORMS_AT) & 15))


def value_heads(shape_):
    f = iota(shape_, 1)
    point = f - H * C
    for _ in range(2):
        point = jnp.where(point >= H * PV, point - H * PV, point)
    return jnp.where(f < H * C, f >> 4, jnp.where(f < SUM_AT, point >> 3, f - SUM_AT))


def row_of(rows, first):
    gap = iota((rows, 128), 0) - H * (iota((rows, 128), 1) - first)
    return jnp.where((gap >= 0) & (gap < H), 1.0, 0.0).astype(BF16)


def fetch_all(pairs, sems):
    copies = [pltpu.make_async_copy(src, dst, sems.at[k]) for k, (src, dst) in enumerate(pairs)]
    for c in copies:
        c.start()
    return copies


def pack_kernel(qs_in, ks_in, krot_in, kanc_in, q_out, k_out, qs, frames, sems):
    own = ks_in.shape[0]
    copies = fetch_all(
        [
            (krot_in, frames.at[pl.ds(0, 9)]),
            (kanc_in, frames.at[pl.ds(16, 3)]),
            (qs_in, qs),
            (ks_in, k_out.at[:, pl.ds(0, D)]),
        ],
        sems,
    )
    copies[0].wait()
    copies[1].wait()
    row = iota((24, own), 0)
    both = jnp.where((row < 9) | ((row >= 16) & (row < 19)), frames[...], 0.0)
    parts = [p.astype(F32) for p in split(both)]
    parts = jnp.concatenate(parts + [jnp.zeros((56, own), F32)], axis=0)
    k_out[:, D:] = parts.T.astype(BF16)
    copies[2].wait()
    for c in range(q_out.shape[0]):
        q_out[c] = qs[...]
    copies[3].wait()


def rotated(rot, anc, local):
    size = local.shape[0] // 3
    part = [local[size * b : size * (b + 1)] for b in range(3)]
    return [
        rot[3 * a : 3 * a + 1] * part[0]
        + rot[3 * a + 1 : 3 * a + 2] * part[1]
        + rot[3 * a + 2 : 3 * a + 3] * part[2]
        + anc[a : a + 1]
        for a in range(3)
    ]


def lane_sums(table, wanted):
    return jnp.sum(jnp.where(wanted, table, 0.0), axis=1, keepdims=True)


def norms_of(points, scale):
    heads = jnp.where(iota((16, H * PQ), 0) == (iota((16, H * PQ), 1) >> 2), 1.0, 0.0)
    by_head = lane_sums(scale, iota((16, H), 0) == iota((16, H), 1))
    squares = points[0] * points[0] + points[1] * points[1] + points[2] * points[2]
    return split(-by_head * dot(heads, squares, precision=PRECISE))


def key_kernel(*refs):
    small_hbm, (w_out, key_out, column_out) = refs[:KEY_SMALL], refs[KEY_SMALL : KEY_SMALL + 3]
    small = refs[KEY_SMALL + 3 : 2 * KEY_SMALL + 3]
    w_pad, key_side, columns, kall, sems, more = refs[2 * KEY_SMALL + 3 :]
    copies = fetch_all(list(zip(small_hbm, small)), sems)
    for c in copies:
        c.wait()
    w, k0, k1, k2, k3, kchain, kw, vw, kpw, vpw, gamma, gap = small
    half = w_pad.shape[1] // 2
    width = w.shape[1]
    w_pad[:, :width] = w[...]
    w_pad[:, width:] = jnp.zeros((w.shape[0], 2 * half - width), BF16)
    core = lax.rem(lax.axis_index("row"), 2)
    mine = pl.ds(pl.multiple_of(core * half, half), half)
    cols = w_out.shape[0]
    stores = fetch_all([(w_pad.at[:, mine], w_out.at[c]) for c in range(cols)], more)

    chips = 4
    here = lax.axis_index("row") // 2
    size = k0.shape[0]
    for d, block in enumerate((k0, k1, k2, k3)):
        at = pl.multiple_of(lax.rem(here + chips - d, chips) * size, size)
        kall[pl.ds(at, size), :] = block[...]

    rows = kall[:, :D]
    keys = kall.shape[0]
    eye = jnp.where(iota((128, 128), 0) == iota((128, 128), 1), 1.0, 0.0).astype(BF16)
    frames = dot(eye, kall[:, D:], 1, 1)
    frames = (frames[0:24] + frames[24:48]) + frames[48:72]
    krot, kanc = frames[0:9], frames[16:19]

    def project(weight):
        return dot(weight[...], rows, 1, 1)

    kpoints = [p.astype(BF16) for p in rotated(krot, kanc, project(kpw))]
    vpoints = [p.astype(BF16) for p in rotated(krot, kanc, project(vpw))]
    apart = jnp.where(iota((16, keys), 0) != kchain[...], 1.0, 0.0).astype(BF16)
    ones = jnp.ones((16, keys), BF16)
    norms = norms_of([p.astype(F32) for p in kpoints], gamma[...] * POINT_SCALE)
    pieces = [project(kw).astype(BF16), apart, apart, apart, *kpoints, *kpoints, *kpoints]
    pieces += [ones, ones, ones, *norms]
    pieces += [project(vw).astype(BF16), *vpoints, ones, jnp.zeros((16, keys), BF16)]
    at = 0
    for piece in pieces:
        key_side[at : at + piece.shape[0]] = piece
        at += piece.shape[0]

    own_gap = lane_sums(gap[...], head_row((RB, H)) == iota((RB, H), 1))
    lane = iota((RB, DEPTH), 1)
    by_column = jnp.where(head_row((RB, DEPTH)) == column_heads(), 1.0, 0.0)
    for t, part in enumerate(split(own_gap)):
        inside = (lane >= CHAIN_AT + 16 * t) & (lane < CHAIN_AT + 16 * (t + 1))
        by_column = jnp.where(inside, part.astype(F32), by_column)
    columns[:, :DEPTH] = by_column
    columns[:, DEPTH:] = jnp.where(head_row((RB, WIDE)) == value_heads((RB, WIDE)), 1.0, 0.0)
    stores.append(pltpu.make_async_copy(key_side, key_out, more.at[cols]))
    stores.append(pltpu.make_async_copy(columns, column_out, more.at[cols + 1]))
    stores[cols].start()
    stores[cols + 1].start()

    for c in stores:
        c.wait()


def attend_kernel(pair_hbm, *refs):
    small_hbm, (out, aux), small = refs[:SMALL], refs[SMALL : SMALL + 2], refs[SMALL + 2 : 2 * SMALL + 2]
    pair, left, logits, attn, extra, pair_sems, sems = refs[2 * SMALL + 2 :]
    qall, qrot, qanc, qchain, qw, qpw, gamma, kmask, pw, columns, key_side = small
    blocks = pair.shape[0] // QB
    copies = fetch_all(list(zip(small_hbm, small)), sems)

    def fetch(b):
        at = pl.ds(QB * b, QB)
        return pltpu.make_async_copy(pair_hbm.at[at], pair.at[at], pair_sems.at[b])

    def start(b):
        if b < blocks:
            fetch(b).start()

    for c in copies[:9]:
        c.wait()
    for b in range(AHEAD):
        start(b)

    scale = gamma[...] * POINT_SCALE
    q = dot(qw[...], qall[...]).astype(BF16).astype(F32) * C ** (-0.5)
    points = rotated(qrot[...], qanc[...], dot(qpw[...], qall[...]))
    by_point = lane_sums(scale, (iota((H * PQ, H), 0) >> 2) == iota((H * PQ, H), 1))
    first, second, third = split(jnp.concatenate([2.0 * by_point * p for p in points], axis=0))
    count = qall.shape[1]
    chain = jnp.where(iota((16, count), 0) == qchain[...], 1.0, 0.0).astype(BF16)
    ones = jnp.ones((16, count), BF16)
    norms = norms_of(points, scale)
    table = jnp.concatenate(
        [q.astype(BF16), chain, chain, chain, first, second, third, *norms, ones, ones, ones], axis=0
    )

    own = iota((QB, 128), 1) == QB * lax.axis_index("col") + iota((QB, 128), 0)
    frame = jnp.zeros((QB, 128), F32)
    for k in range(12):
        value = lane_sums(qrot[k : k + 1] if k < 9 else qanc[k - 9 : k - 8], own)
        frame = jnp.where(iota((QB, 128), 1) == k, value, frame)
    aux[:, :D] = dot(jnp.where(own, 1.0, 0.0).astype(BF16), qall[...], 1, 1)
    aux[:, D:] = frame

    copies[9].wait()
    by_column = columns[:, :DEPTH]
    tall = TALL * RB
    for g in range(blocks // TALL):
        spread = dot(row_of(tall, TALL * QB * g), table, 1, 1)
        for t in range(TALL):
            at = tall * g + RB * t
            left[at : at + RB] = (spread[RB * t : RB * (t + 1)] * by_column).astype(BF16)
    copies[10].wait()
    done = 0
    for g in range(blocks // TALL):
        logits[tall * g : tall * (g + 1)] = dot(left[tall * g : tall * (g + 1)], key_side[:DEPTH])
        for _ in range(TALL // 2):
            fetch(done).wait()
            start(done + AHEAD)
            done += 1

    pick = iota((2 * H, H), 0) - iota((2 * H, H), 1)
    pick = jnp.where((pick == 0) | (pick == H), 1.0, 0.0).astype(BF16)
    turned = dot(pick, pw[...])
    upper = iota((2 * H, CZ), 0) < H
    weights = jnp.concatenate(
        [jnp.where(upper, turned, 0.0), jnp.where(upper, 0.0, turned)], axis=1
    ).astype(BF16)

    real = kmask[...] > 0
    at_head = jnp.where(head_row((RB, 128)) == iota((RB, 128), 1), 1.0, 0.0)
    lanes = [at_head] + [pltpu.roll(at_head, 16 * t, 1) for t in range(1, 4)]

    def both(b, p):
        i = QB * b + 2 * p
        return jnp.concatenate([pair[i], pair[i + 1]], axis=1)

    def bias_of(b):
        return [dot(weights, both(b, p), 1, 1) for p in range(QB // 2)]

    for b in range(blocks):
        if b >= done:
            fetch(b).wait()
            start(b + AHEAD)
        for p in range(QB // 2):
            i = QB * b + 2 * p
            logits[H * i : H * (i + 2)] += dot(weights, both(b, p), 1, 1)
    for b in range(blocks):
        at = slice(RB * b, RB * (b + 1))
        x = jnp.where(real, LOGIT_SCALE * logits[at], MASKED)
        top = jnp.max(x, axis=1, keepdims=True)
        e = jnp.exp(x - top)
        attn[at] = e.astype(BF16)
        tops = [p.astype(F32) for p in split(top)]
        extra[at] = tops[0] * lanes[0] + tops[1] * lanes[1] + tops[2] * lanes[2]
        parts = []
        for p in range(QB // 2):
            z = dot(e[2 * H * p : 2 * H * (p + 1)].astype(BF16), both(b, p))
            parts.append(jnp.where(upper, z[:, :CZ], z[:, CZ:]))
        out[b, :RB] = jnp.concatenate(parts, axis=0).astype(BF16)

    by_lane = columns[:, DEPTH:]
    own = iota((QB, RB), 1) - H * iota((QB, RB), 0)
    own = jnp.where((own >= 0) & (own < H), 1.0, 0.0).astype(BF16)
    for g in range(blocks // TALL):
        wide = dot(attn[tall * g : tall * (g + 1)], key_side[DEPTH:], 1, 1)
        for s in range(TALL):
            b = TALL * g + s
            mine = wide[RB * s : RB * (s + 1)] * by_lane
            rounded = mine.astype(BF16)
            last = mine[:, 384:] - rounded[:, 384:].astype(F32)
            rest = extra[RB * b : RB * (b + 1)] + pltpu.roll(last, 80, 1) * lanes[3]
            packed = dot(own, rounded)
            tail = dot(own, rest.astype(BF16))
            out[b, RB:] = jnp.concatenate(
                [packed[:, 128 * t : 128 * (t + 1)] for t in range(4)]
                + [tail, jnp.zeros((8, 128), F32)],
                axis=0,
            ).astype(BF16)


def finish_kernel(cols, got, w_mine, w_other, aux, out, rows, halves):
    spread = jnp.where(iota((128, WIDE), 0) == value_heads((128, WIDE)), 1.0, 0.0).astype(BF16)
    at_head = jnp.where(head_row((RB, 128)) == iota((RB, 128), 1), 1.0, 0.0)
    tail = got[:, RB:, :].astype(F32)
    count = cols * QB

    def tile(t):
        return tail[:, QB * t : QB * (t + 1)].reshape(count, 128)

    marks = tile(4)
    top = (marks + pltpu.roll(marks, 112, 1)) + pltpu.roll(marks, 96, 1)
    sums = pltpu.roll(tile(3), 32, 1) + pltpu.roll(marks, 80, 1)
    top = top.reshape(cols, QB, 128)
    factor = jnp.exp(top - jnp.max(top, axis=0, keepdims=True))
    total = jnp.sum(sums.reshape(cols, QB, 128) * factor, axis=0, keepdims=True)
    head = iota((cols, QB, 128), 2) < H
    factor = jnp.where(head, factor / total, 0.0).reshape(count, 128)
    high, low, _ = split(factor)
    wide = dot(high, spread) + dot(low, spread)
    averaged = [
        jnp.sum((tile(t) * wide[:, 128 * t : 128 * (t + 1)]).reshape(cols, QB, 128), axis=0)
        for t in range(4)
    ]
    averaged = jnp.concatenate(averaged, axis=1)

    z = jnp.zeros((RB, CZ), F32)
    for c in range(cols):
        pick = row_of(RB, QB * c)
        mine = (dot(pick, high) + dot(pick, low)) * at_head
        z = z + got[c, :RB].astype(F32) * jnp.sum(mine, axis=1, keepdims=True)
    rows[...] = z

    def mine(k):
        return aux[:, D + k : D + k + 1]

    cut = H * C
    step = H * PV
    shifted = [averaged[:, cut + step * b : cut + step * (b + 1)] - mine(9 + b) for b in range(3)]
    local = [
        mine(a) * shifted[0] + mine(3 + a) * shifted[1] + mine(6 + a) * shifted[2]
        for a in range(3)
    ]
    features = []
    for h in range(H):
        features.append(averaged[:, C * h : C * (h + 1)])
        features += [x[:, PV * h : PV * (h + 1)] for x in local]
        features.append(rows[pl.ds(h, QB, stride=H), :])
    features.append(jnp.zeros((QB, 2 * HALF - H * FEAT), F32))
    features = jnp.concatenate(features, axis=1)
    halves[0], halves[1] = features[:, :HALF], features[:, HALF:]
    core = lax.rem(lax.axis_index("row"), 2)
    mixed = dot(halves[core].astype(BF16), w_mine[...], 1, 1)
    mixed = mixed + dot(halves[1 - core].astype(BF16), w_other[...], 1, 1)
    mixed = aux[:, :D] + mixed
    centred = mixed - jnp.sum(mixed, axis=1, keepdims=True) * (1.0 / D)
    variance = jnp.sum(centred * centred, axis=1, keepdims=True) * (1.0 / D)
    normal = centred * lax.rsqrt(variance + NORM_EPS)
    width = D // cols
    out[...] = jnp.zeros(out.shape, F32)
    for c in range(cols):
        out[c, :, :width] = normal[:, width * c : width * (c + 1)]


def scale_kernel(normal, gain, shift, out):
    width = gain.shape[1]
    y = normal[...][:, :width] * gain[...] + shift[...]
    out[...] = y.T.astype(BF16)


HBM = pl.BlockSpec(memory_space=pltpu.HBM)
VMEM = pl.BlockSpec(memory_space=pltpu.VMEM)
PARAMS = pltpu.CompilerParams(vmem_limit_bytes=VMEM_BYTES)
SMALL_PARAMS = pltpu.CompilerParams(vmem_limit_bytes=16 << 20)


def shape(dims, dtype):
    return jax.ShapeDtypeStruct(dims, dtype)


def held(arrays):
    return [pltpu.VMEM(x.shape, x.dtype) for x in arrays]


def signals(count):
    return pltpu.SemaphoreType.DMA((count,))


def cost(pair, times):
    return pl.CostEstimate(
        flops=2 * times * pair.size * 128, bytes_accessed=2 * times * pair.size, transcendentals=0
    )


def pack(cols, query_single, key_single, key_rotation, key_anchor):
    own = key_single.shape[0]
    return pl.pallas_call(
        pack_kernel,
        in_specs=[HBM] * 4,
        out_specs=[VMEM, VMEM],
        out_shape=[shape((cols,) + query_single.shape, BF16), shape((own, D + 128), BF16)],
        scratch_shapes=held([query_single]) + [pltpu.VMEM((24, own), F32), signals(4)],
        compiler_params=PARAMS,
    )(query_single, key_single, key_rotation, key_anchor)


def key_parts(cols, out_weight, *small):
    keys = small[4].shape[1]
    width = out_weight.shape[0]
    results = [
        shape((cols, width, HALF), BF16),
        shape((DEPTH + WIDE, keys), BF16),
        shape((RB, DEPTH + WIDE), F32),
    ]
    return pl.pallas_call(
        key_kernel,
        in_specs=[HBM] * KEY_SMALL,
        out_specs=[HBM] * 3,
        out_shape=results,
        scratch_shapes=held((out_weight,) + small)
        + [pltpu.VMEM((width, 2 * HALF), BF16)]
        + held(results[1:])
        + [pltpu.VMEM((keys, D + 128), BF16), signals(KEY_SMALL), signals(2 + cols)],
        compiler_params=PARAMS,
        cost_estimate=pl.CostEstimate(
            flops=2 * D * keys * 1024, bytes_accessed=16 << 20, transcendentals=0
        ),
    )(out_weight, *small)


def attend(pair, *small):
    blocks, keys = pair.shape[0] // QB, pair.shape[1]
    return pl.pallas_call(
        attend_kernel,
        in_specs=[HBM] * (1 + SMALL),
        out_specs=[VMEM, VMEM],
        out_shape=[shape((blocks, CHUNK, 128), BF16), shape((QB, D + 128), F32)],
        scratch_shapes=held(small)
        + held([pair])
        + [
            pltpu.VMEM((blocks * RB, DEPTH), BF16),
            pltpu.VMEM((blocks * RB, keys), F32),
            pltpu.VMEM((blocks * RB, keys), BF16),
            pltpu.VMEM((blocks * RB, 128), F32),
            signals(blocks),
            signals(SMALL),
        ],
        compiler_params=PARAMS,
        cost_estimate=cost(pair, 3),
    )(pair, *small)


def finish(cols, *taken):
    return pl.pallas_call(
        lambda *refs: finish_kernel(cols, *refs),
        in_specs=[VMEM] * 4,
        out_specs=VMEM,
        out_shape=shape((cols, QB, 128), F32),
        scratch_shapes=[pltpu.VMEM((RB, CZ), F32), pltpu.VMEM((2, QB, HALF), F32)],
        compiler_params=SMALL_PARAMS,
    )(*taken)


def scale(*taken):
    width, queries = taken[1].shape[1], taken[0].shape[0]
    return pl.pallas_call(
        scale_kernel,
        in_specs=[VMEM] * 3,
        out_specs=VMEM,
        out_shape=shape((width, queries), BF16),
        compiler_params=SMALL_PARAMS,
    )(*taken)


def on_device(
    query_single,
    query_rotation,
    query_anchor,
    query_chain,
    key_single,
    key_rotation,
    key_anchor,
    key_chain,
    key_mask,
    pair_tile,
    query_weight,
    query_point_weight,
    key_weight,
    value_weight,
    key_point_weight,
    value_point_weight,
    pair_weight,
    head_gamma,
    chain_gap,
    out_weight,
    norm_gain,
    norm_shift,
):
    cols = lax.axis_size("col")

    def send(x):
        return lax.all_to_all(x, "col", 0, 0)

    q_pack, k_pack = pack(cols, query_single.T, key_single, key_rotation, key_anchor)
    cores = [[2 * x, 2 * x + 1] for x in range(4)]
    k_pack = lax.all_gather(k_pack, "row", axis=0, tiled=True, axis_index_groups=cores)
    k_others = [
        lax.ppermute(k_pack, "row", [(r, (r + 2 * d) % 8) for r in range(8)]) for d in (1, 2, 3)
    ]
    qall = send(q_pack).reshape(D, -1)
    gamma = head_gamma.reshape(1, -1)
    w_pack, key_side, columns = key_parts(
        cols,
        out_weight.T,
        k_pack,
        *k_others,
        key_chain.reshape(1, -1),
        key_weight.T,
        value_weight.T,
        key_point_weight.T,
        value_point_weight.T,
        gamma,
        chain_gap.reshape(1, -1),
    )
    weights = send(w_pack).reshape(D, HALF)
    parts, aux = attend(
        pair_tile,
        qall,
        query_rotation,
        query_anchor,
        query_chain.reshape(1, -1),
        query_weight.T,
        query_point_weight.T,
        gamma,
        key_mask.reshape(1, -1),
        pair_weight.T,
        columns,
        key_side,
    )
    parts, weights = lax.optimization_barrier((parts, weights))
    w_other = lax.ppermute(weights, "row", [(r, r ^ 1) for r in range(8)])
    normal = finish(cols, send(parts), weights, w_other, aux)
    normal = send(normal).reshape(-1, 128)
    return scale(normal, norm_gain.reshape(1, -1), norm_shift.reshape(1, -1)).T


def solution(mesh):
    placed = (
        P("row", "col"),
        P(None, "row"),
        P(None, "row"),
        P("row"),
        P(("col", "row"), None),
        P(None, ("col", "row")),
        P(None, ("col", "row")),
        P("col"),
        P("col"),
        P("row", "col", None),
        P(),
        P(),
        P(),
        P(),
        P(),
        P(),
        P(),
        P(),
        P(),
        P(None, "col"),
        P("col"),
        P("col"),
    )
    return jax.shard_map(
        on_device, mesh=mesh, in_specs=placed, out_specs=P("row", "col"), check_vma=False
    )
```

time: 297 us -> 79.4 us (0.27)
  blocking collectives: 187 us -> 33.1 us
  waiting for transfers between devices: 45.8 us -> 2.95 us
  matrix products: 32.3 us -> 0 us
  Pallas kernels: 0 us -> 23.7 us
  starting transfers between devices: 0.01 us -> 17.5 us
  between operations: 13.9 us -> 0.14 us
  other arithmetic: 10.3 us -> 0 us
  local copies, waits for them, and re-layouts: 6.7 us -> 1.44 us
    psum x3 -> x0, blocking collectives: 109 us -> none  [the longest x1 38.2 us: on_device(): average = lax.psum(jnp.sum(mixed, axis=1), 'col') / D]
    psum x1 -> x0, waiting for transfers between devices: 45.8 us -> none  [on_device(): lax.psum((numerators * factor[:, None, :]).astype(jnp.bfloat16), 'col')]
    pmax x1 -> x0, blocking collectives: 38.8 us -> none  [on_device(): highest = lax.pmax(maximum, 'col')]
    all_gather x2 -> x1, blocking collectives: 39.1 us -> 2.11 us  [on_device(): lax.all_gather(k_pack, 'row', axis=0, tiled=True, axis_index_groups=cores)]
    dot_general x9 -> x0, matrix products: 32.3 us -> none  [the longest x1 12.2 us: block_partials(): jnp.einsum('qkc,ch->hqk', pair, pair_weight, preferred_element_type=jnp.f...]
    all_to_all x0 -> x2, blocking collectives: none -> 31 us  [send(): return lax.all_to_all(x, 'col', 0, 0)]
    pallas_call x0 -> x5, Pallas kernels: none -> 23.7 us  [the longest x1 15.8 us: attend(): pl.pallas_call(attend_kernel, in_specs=[HBM] * (1 + SMALL), out_specs=[VM...]
    all_to_all x0 -> x2, starting transfers between devices: none -> 12.9 us  [send(): return lax.all_to_all(x, 'col', 0, 0)]
  transfers between devices with their start and end apart: 1 -> 6, of which waited for: 1 -> 1; matrix products, arithmetic and copies ran while one was open for 0% -> 0% of each run, Pallas kernels for 0% -> 25%
where the time goes in v2:
time: 79.4 us; the launch traced here: 78.8 us
  blocking collectives  33.1 us (42%)
  Pallas kernels  23.7 us (30%)
  starting transfers between devices  17.5 us (22%)
  waiting for transfers between devices  2.95 us (4%)
  local copies, waits for them, and re-layouts  1.44 us (2%)
    all_to_all x2, blocking collectives, send(): return lax.all_to_all(x, 'col', 0, 0)  31 us
    pallas_call x1, Pallas kernels, attend(): pl.pallas_call(attend_kernel, in_specs=[HBM] * (1 + SMALL), out_specs=[VM...  15.8 us
    all_to_all x2, starting transfers between devices, send(): return lax.all_to_all(x, 'col', 0, 0)  12.9 us
    ppermute x3, starting transfers between devices, on_device(): lax.ppermute(k_pack, 'row', [(r, (r + 2 * d) % 8) for r in range(8)])  4.55 us
    pallas_call x1, Pallas kernels, key_parts(): pl.pallas_call(key_kernel, in_specs=[HBM] * KEY_SMALL, out_specs=[HBM] *...  4.03 us
    all_to_all x2, waiting for transfers between devices, send(): return lax.all_to_all(x, 'col', 0, 0)  2.93 us
    all_gather x1, blocking collectives, on_device(): lax.all_gather(k_pack, 'row', axis=0, tiled=True, axis_index_groups=cores)  2.11 us
    pallas_call x1, Pallas kernels, pack(): pl.pallas_call(pack_kernel, in_specs=[HBM] * 4, out_specs=[VMEM, VMEM], o...  1.59 us
  transfers between devices with their start and end apart: 6, of which 1 were waited for; matrix products, arithmetic and copies ran while one was open for 0% of the time, Pallas kernels for 25%

profile of v2, /device:TPU:0, one launch (start us, length us, event | category | flops | bytes accessed | tf_op | source)
XLA Modules:
  0.0 78.8 jit_solution(8552923187946826025)
XLA Ops:
  0.0 0.0 copy-start.2
  0.0 0.0 copy-start.1
  0.0 1.6 %shard_map.208 = (bf16[16,24,128]{2,1,0:T(8,128)(2,1)}, bf16[64,512]{1,0:T(8,128)(2,1)}) custom-call(bf16[24,128]{1,0:T(8,128)(2,1)} %bitcast.26, bf16[64,384]{1,0:T(8,128)(2,1)} %ks_in.1, f32[9,64]{1,0:T(8,128)} %krot_in.1, f32[3,64]{1,0:T(4,128)} %kanc_in.1), custom_call_target="tpu_custom_call" | custom-call | tf_op jit(solution)/shard_map/pallas_call | solution.py:417
  1.6 2.1 %all_gather.3.refs_1_ = bf16[128,512]{1,0:T(8,128)(2,1)S(1)} all-gather(bf16[64,512]{1,0:T(8,128)(2,1)} %get-tuple-element.15), channel_id=1, replica_groups={{0,16},{32,48},{64,80},{96,112},{1,17},{33,49},{65,81},{97,113},{2,18},..., dimensions={0}, use_global_device_ids=true | all-gather | bytes 196608 | tf_op jit(solution)/shard_map/all_gather | solution.py:526
  3.7 0.0 copy-start.3
  3.7 2.9 %collective-permute-start.2 = (bf16[128,512]{1,0:T(8,128)(2,1)S(1)}, bf16[128,512]{1,0:T(8,128)(2,1)S(1)}, u32[]{:S(2)}, u32[]{:S(2)}) collective-permute-start(bf16[128,512]{1,0:T(8,128)(2,1)S(1)} %all_gather.3.refs_1_), channel_id=1, source_target_pairs={{0,96},{16,112},{32,0},{48,16},{64,32},{80,48},{96,64},{112,80},{1... | collective-permute-start | bytes 393224 | tf_op jit(solution)/shard_map/ppermute | solution.py:528
  6.6 0.8 %collective-permute-start.1 = (bf16[128,512]{1,0:T(8,128)(2,1)S(1)}, bf16[128,512]{1,0:T(8,128)(2,1)S(1)}, u32[]{:S(2)}, u32[]{:S(2)}) collective-permute-start(bf16[128,512]{1,0:T(8,128)(2,1)S(1)} %all_gather.3.refs_1_), channel_id=1, source_target_pairs={{0,64},{16,80},{32,96},{48,112},{64,0},{80,16},{96,32},{112,48},{1... | collective-permute-start | bytes 393224 | tf_op jit(solution)/shard_map/ppermute | solution.py:528
  7.4 0.9 %collective-permute-start = (bf16[128,512]{1,0:T(8,128)(2,1)S(1)}, bf16[128,512]{1,0:T(8,128)(2,1)S(1)}, u32[]{:S(2)}, u32[]{:S(2)}) collective-permute-start(bf16[128,512]{1,0:T(8,128)(2,1)S(1)} %all_gather.3.refs_1_), channel_id=1, source_target_pairs={{0,32},{16,48},{32,64},{48,80},{64,96},{80,112},{96,0},{112,16},{1... | collective-permute-start | bytes 393224 | tf_op jit(solution)/shard_map/ppermute | solution.py:528
  8.3 8.0 %all-to-all-start = ((bf16[16,24,128]{2,1,0:T(8,128)(2,1)}), bf16[16,24,128]{2,1,0:T(8,128)(2,1)S(1)}, u32[]{:S(2)}, u32[]{:S(2)}) async-start(bf16[16,24,128]{2,1,0:T(8,128)(2,1)} %get-tuple-element.14), calls=%async_computation | async-start | bytes 196608 | tf_op jit(solution)/shard_map/all_to_all | solution.py:522
  16.3 0.0 collective-permute-done.2.refs_4_
  16.3 0.0 copy-start.5
  16.3 0.0 collective-permute-done.1.refs_3_
  16.4 0.0 copy-start.6
  16.4 0.0 collective-permute-done.refs_2_
  16.4 0.0 copy-start.7
  16.4 0.0 copy-done.3
  16.4 0.6 copy-done.5
  17.0 0.1 copy-done.6
  17.0 0.1 copy-done.7
  17.1 4.0 %shard_map.209 = (bf16[16,24,1024]{2,1,0:T(8,128)(2,1)}, bf16[1280,512]{1,0:T(8,128)(2,1)}, f32[96,1280]{1,0:T(8,128)}) custom-call(bf16[24,2016]{1,0:T(8,128)(2,1)} %bitcast.33, bf16[128,512]{1,0:T(8,128)(2,1)} %copy-done.3, bf16[128,512]{1,0:T(8,128)(2,1)} %copy-done.7, bf16[128,512]{1,0:T(8,128)(2,1)} %copy-done.6, bf16[128,512]{1,0:T(8,128)(2,1)} %copy-done.5, ...), custom_call_target="tpu_custom_call" | custom-call | flops 402653184 | bytes 16777216 | tf_op jit(solution)/shard_map/pallas_call | solution.py:435
  21.1 2.9 %all-to-all-done = bf16[16,24,128]{2,1,0:T(8,128)(2,1)S(1)} async-done(((bf16[16,24,128]{2,1,0:T(8,128)(2,1)}), bf16[16,24,128]{2,1,0:T(8,128)(2,1)S(1)}, u32[]{:S(2)}, u32[]{:S(2)}) %all-to-all-start) | async-done | bytes 98336 | tf_op jit(solution)/shard_map/all_to_all | solution.py:522
  24.1 0.0 copy-start.4
  24.1 4.8 %all-to-all-start.1 = ((bf16[16,24,1024]{2,1,0:T(8,128)(2,1)}), bf16[16,24,1024]{2,1,0:T(8,128)(2,1)S(1)}, u32[]{:S(2)}, u32[]{:S(2)}) async-start(bf16[16,24,1024]{2,1,0:T(8,128)(2,1)} %get-tuple-element.19), calls=%async_computation.1 | async-start | bytes 1572864 | tf_op jit(solution)/shard_map/all_to_all | solution.py:522
  28.9 0.0 copy-done.4
  28.9 15.8 %shard_map.210 = (bf16[16,144,128]{2,1,0:T(8,128)(2,1)}, f32[8,512]{1,0:T(8,128)}) custom-call(bf16[128,512,128]{2,1,0:T(8,128)(2,1)} %pair_hbm.1, bf16[384,128]{1,0:T(8,128)(2,1)} %bitcast.25, f32[9,128]{1,0:T(8,128)} %refs_1_.1, f32[3,128]{1,0:T(4,128)} %refs_2_.1, s32[1,128]{1,0:T(1,128)} %bitcast.38, bf16[192,384]{1,0:T(8,128)(2,1)} %bitcast.30, ...), custom_call_target="tpu_custom_call" | custom-call | flops 6442450944 | bytes 50331648 | tf_op jit(solution)/shard_map/pallas_call | solution.py:453
  44.8 0.0 all-to-all-done.1
  44.8 0.1 collective-permute-start.3
  44.9 20.1 %all_to_all.20.refs_0_ = bf16[16,144,128]{2,1,0:T(8,128)(2,1)S(1)} all-to-all(bf16[16,144,128]{2,1,0:T(8,128)(2,1)} %get-tuple-element.20), channel_id=1, replica_groups=mesh['row'=8,'col'=16] {'col'}, dimensions={0} | all-to-all | bytes 1179648 | tf_op jit(solution)/shard_map/all_to_all | solution.py:522
  65.0 0.0 collective-permute-done.3.refs_2_
  65.0 0.0 copy-start
  65.0 0.7 copy-done
  65.7 1.5 %shard_map.211 = f32[16,8,128]{2,1,0:T(8,128)S(1)} custom-call(bf16[16,144,128]{2,1,0:T(8,128)(2,1)S(1)} %all_to_all.20.refs_0_, bf16[384,1024]{1,0:T(8,128)(2,1)S(1)} %bitcast.21, bf16[384,1024]{1,0:T(8,128)(2,1)S(1)} %collective-permute-done.3.refs_2_, f32[8,512]{1,0:T(8,128)S(1)} %copy-done), custom_call_target="tpu_custom_call" | custom-call | tf_op jit(solution)/shard_map/pallas_call | solution.py:474
  67.3 10.9 %all_to_all.21 = f32[16,8,128]{2,1,0:T(8,128)S(1)} all-to-all(f32[16,8,128]{2,1,0:T(8,128)S(1)} %shard_map.211), channel_id=1, replica_groups=mesh['row'=8,'col'=16] {'col'}, dimensions={0} | all-to-all | bytes 131072 | tf_op jit(solution)/shard_map/all_to_all | solution.py:522
  78.2 0.0 copy-done.2
  78.2 0.0 copy-done.1
  78.2 0.7 shard_map.212
Async XLA Ops:
  0.0 78.2 %copy-start.2 = (f32[24]{0:T(128)S(1)}, f32[24]{0:T(128)}, u32[]{:S(2)}) copy-start(f32[24]{0:T(128)} %param.43) | copy-start | bytes 292
  0.0 78.2 %copy-start.1 = (f32[24]{0:T(128)S(1)}, f32[24]{0:T(128)}, u32[]{:S(2)}) copy-start(f32[24]{0:T(128)} %param.42) | copy-start | bytes 292
  3.7 12.7 %copy-start.3 = (bf16[128,512]{1,0:T(8,128)(2,1)}, bf16[128,512]{1,0:T(8,128)(2,1)S(1)}, u32[]{:S(2)}) copy-start(bf16[128,512]{1,0:T(8,128)(2,1)S(1)} %all_gather.3.refs_1_) | copy-start | bytes 393220
  3.7 12.6 %collective-permute-start.2 = (bf16[128,512]{1,0:T(8,128)(2,1)S(1)}, bf16[128,512]{1,0:T(8,128)(2,1)S(1)}, u32[]{:S(2)}, u32[]{:S(2)}) collective-permute-start(bf16[128,512]{1,0:T(8,128)(2,1)S(1)} %all_gather.3.refs_1_), channel_id=1, source_target_pairs={{0,96},{16,112},{32,0},{48,16},{64,32},{80,48},{96,64},{112,80},{1... | collective-permute-start | bytes 393224 | tf_op jit(solution)/shard_map/ppermute | solution.py:528
  6.6 9.8 %collective-permute-start.1 = (bf16[128,512]{1,0:T(8,128)(2,1)S(1)}, bf16[128,512]{1,0:T(8,128)(2,1)S(1)}, u32[]{:S(2)}, u32[]{:S(2)}) collective-permute-start(bf16[128,512]{1,0:T(8,128)(2,1)S(1)} %all_gather.3.refs_1_), channel_id=1, source_target_pairs={{0,64},{16,80},{32,96},{48,112},{64,0},{80,16},{96,32},{112,48},{1... | collective-permute-start | bytes 393224 | tf_op jit(solution)/shard_map/ppermute | solution.py:528
  7.4 9.0 %collective-permute-start = (bf16[128,512]{1,0:T(8,128)(2,1)S(1)}, bf16[128,512]{1,0:T(8,128)(2,1)S(1)}, u32[]{:S(2)}, u32[]{:S(2)}) collective-permute-start(bf16[128,512]{1,0:T(8,128)(2,1)S(1)} %all_gather.3.refs_1_), channel_id=1, source_target_pairs={{0,32},{16,48},{32,64},{48,80},{64,96},{80,112},{96,0},{112,16},{1... | collective-permute-start | bytes 393224 | tf_op jit(solution)/shard_map/ppermute | solution.py:528
  8.3 15.8 %all-to-all-start = ((bf16[16,24,128]{2,1,0:T(8,128)(2,1)}), bf16[16,24,128]{2,1,0:T(8,128)(2,1)S(1)}, u32[]{:S(2)}, u32[]{:S(2)}) async-start(bf16[16,24,128]{2,1,0:T(8,128)(2,1)} %get-tuple-element.14), calls=%async_computation | async-start | bytes 196608 | tf_op jit(solution)/shard_map/all_to_all | solution.py:522
  16.3 0.7 copy-start.5
  16.4 0.7 copy-start.6
  16.4 0.7 copy-start.7
  24.1 4.9 %copy-start.4 = (bf16[16,24,128]{2,1,0:T(8,128)(2,1)}, bf16[16,24,128]{2,1,0:T(8,128)(2,1)S(1)}, u32[]{:S(2)}) copy-start(bf16[16,24,128]{2,1,0:T(8,128)(2,1)S(1)} %all-to-all-done) | copy-start | bytes 294916
  24.1 20.7 %all-to-all-start.1 = ((bf16[16,24,1024]{2,1,0:T(8,128)(2,1)}), bf16[16,24,1024]{2,1,0:T(8,128)(2,1)S(1)}, u32[]{:S(2)}, u32[]{:S(2)}) async-start(bf16[16,24,1024]{2,1,0:T(8,128)(2,1)} %get-tuple-element.19), calls=%async_computation.1 | async-start | bytes 1572864 | tf_op jit(solution)/shard_map/all_to_all | solution.py:522
  44.8 20.2 %collective-permute-start.3 = (bf16[384,1024]{1,0:T(8,128)(2,1)S(1)}, bf16[384,1024]{1,0:T(8,128)(2,1)S(1)}, u32[]{:S(2)}, u32[]{:S(2)}) collective-permute-start(bf16[384,1024]{1,0:T(8,128)(2,1)S(1)} %bitcast.20), channel_id=1, source_target_pairs={{0,16},{16,0},{32,48},{48,32},{64,80},{80,64},{96,112},{112,96},{1... | collective-permute-start | bytes 2359304 | tf_op jit(solution)/shard_map/ppermute | solution.py:561
  65.0 0.7 copy-start

commit v3 on v2

--- a/solution.py
+++ b/solution.py
@@ -32,7 +32,7 @@
 VMEM_BYTES = 63_400_000
 SMALL = 11
 KEY_SMALL = 12
-AHEAD = 8
+AHEAD = 12
 TALL = 8
 HALF = 1024
 CHUNK = RB + 48
@@ -203,10 +203,10 @@
 
 def attend_kernel(pair_hbm, *refs):
     small_hbm, (out, aux), small = refs[:SMALL], refs[SMALL : SMALL + 2], refs[SMALL + 2 : 2 * SMALL + 2]
-    pair, left, logits, attn, extra, pair_sems, sems = refs[2 * SMALL + 2 :]
-    qall, qrot, qanc, qchain, qw, qpw, gamma, kmask, pw, columns, key_side = small
+    pair, left, logits, bias, attn, extra, pair_sems, sems = refs[2 * SMALL + 2 :]
+    pw, qall, qrot, qanc, qchain, qw, qpw, gamma, kmask, columns, key_side = small
     blocks = pair.shape[0] // QB
-    copies = fetch_all(list(zip(small_hbm, small)), sems)
+    copies = fetch_all(list(zip(small_hbm, small))[:1], sems)
 
     def fetch(b):
         at = pl.ds(QB * b, QB)
@@ -216,10 +216,32 @@
         if b < blocks:
             fetch(b).start()
 
-    for c in copies[:9]:
-        c.wait()
     for b in range(AHEAD):
         start(b)
+    copies += fetch_all(list(zip(small_hbm, small))[1:], sems.at[pl.ds(1, SMALL - 1)])
+    copies[0].wait()
+
+    pick = iota((2 * H, H), 0) - iota((2 * H, H), 1)
+    pick = jnp.where((pick == 0) | (pick == H), 1.0, 0.0).astype(BF16)
+    turned = dot(pick, pw[...])
+    upper = iota((2 * H, CZ), 0) < H
+    weights = jnp.concatenate(
+        [jnp.where(upper, turned, 0.0), jnp.where(upper, 0.0, turned)], axis=1
+    ).astype(BF16)
+
+    def both(b, p):
+        i = QB * b + 2 * p
+        return jnp.concatenate([pair[i], pair[i + 1]], axis=1)
+
+    for b in range(blocks):
+        fetch(b).wait()
+        start(b + AHEAD)
+        for p in range(QB // 2):
+            i = QB * b + 2 * p
+            bias[H * i : H * (i + 2)] = dot(weights, both(b, p), 1, 1)
+
+    for c in copies[1:]:
+        c.wait()
 
     scale = gamma[...] * POINT_SCALE
     q = dot(qw[...], qall[...]).astype(BF16).astype(F32) * C ** (-0.5)
@@ -242,7 +264,6 @@
     aux[:, :D] = dot(jnp.where(own, 1.0, 0.0).astype(BF16), qall[...], 1, 1)
     aux[:, D:] = frame
 
-    copies[9].wait()
     by_column = columns[:, :DEPTH]
     tall = TALL * RB
     for g in range(blocks // TALL):
@@ -250,54 +271,32 @@
         for t in range(TALL):
             at = tall * g + RB * t
             left[at : at + RB] = (spread[RB * t : RB * (t + 1)] * by_column).astype(BF16)
-    copies[10].wait()
-    done = 0
     for g in range(blocks // TALL):
         logits[tall * g : tall * (g + 1)] = dot(left[tall * g : tall * (g + 1)], key_side[:DEPTH])
-        for _ in range(TALL // 2):
-            fetch(done).wait()
-            start(done + AHEAD)
-            done += 1
-
-    pick = iota((2 * H, H), 0) - iota((2 * H, H), 1)
-    pick = jnp.where((pick == 0) | (pick == H), 1.0, 0.0).astype(BF16)
-    turned = dot(pick, pw[...])
-    upper = iota((2 * H, CZ), 0) < H
-    weights = jnp.concatenate(
-        [jnp.where(upper, turned, 0.0), jnp.where(upper, 0.0, turned)], axis=1
-    ).astype(BF16)
 
     real = kmask[...] > 0
     at_head = jnp.where(head_row((RB, 128)) == iota((RB, 128), 1), 1.0, 0.0)
     lanes = [at_head] + [pltpu.roll(at_head, 16 * t, 1) for t in range(1, 4)]
 
-    def both(b, p):
-        i = QB * b + 2 * p
-        return jnp.concatenate([pair[i], pair[i + 1]], axis=1)
-
-    def bias_of(b):
-        return [dot(weights, both(b, p), 1, 1) for p in range(QB // 2)]
-
-    for b in range(blocks):
-        if b >= done:
-            fetch(b).wait()
-            start(b + AHEAD)
-        for p in range(QB // 2):
-            i = QB * b + 2 * p
-            logits[H * i : H * (i + 2)] += dot(weights, both(b, p), 1, 1)
-    for b in range(blocks):
+    def weigh(b):
         at = slice(RB * b, RB * (b + 1))
-        x = jnp.where(real, LOGIT_SCALE * logits[at], MASKED)
+        x = jnp.where(real, LOGIT_SCALE * (logits[at] + bias[at]), MASKED)
         top = jnp.max(x, axis=1, keepdims=True)
         e = jnp.exp(x - top)
         attn[at] = e.astype(BF16)
         tops = [p.astype(F32) for p in split(top)]
         extra[at] = tops[0] * lanes[0] + tops[1] * lanes[1] + tops[2] * lanes[2]
+        return [e[2 * H * p : 2 * H * (p + 1)].astype(BF16) for p in range(QB // 2)]
+
+    e = weigh(0)
+    for b in range(blocks):
+        later = weigh(b + 1) if b + 1 < blocks else None
         parts = []
         for p in range(QB // 2):
-            z = dot(e[2 * H * p : 2 * H * (p + 1)].astype(BF16), both(b, p))
+            z = dot(e[p], both(b, p))
             parts.append(jnp.where(upper, z[:, :CZ], z[:, CZ:]))
         out[b, :RB] = jnp.concatenate(parts, axis=0).astype(BF16)
+        e = later
 
     by_lane = columns[:, DEPTH:]
     own = iota((QB, RB), 1) - H * iota((QB, RB), 0)
@@ -460,6 +459,7 @@
         + [
             pltpu.VMEM((blocks * RB, DEPTH), BF16),
             pltpu.VMEM((blocks * RB, keys), F32),
+            pltpu.VMEM((blocks * RB, keys), F32),
             pltpu.VMEM((blocks * RB, keys), BF16),
             pltpu.VMEM((blocks * RB, 128), F32),
             signals(blocks),
@@ -545,6 +545,7 @@
     weights = send(w_pack).reshape(D, HALF)
     parts, aux = attend(
         pair_tile,
+        pair_weight.T,
         qall,
         query_rotation,
         query_anchor,
@@ -553,7 +554,6 @@
         query_point_weight.T,
         gamma,
         key_mask.reshape(1, -1),
-        pair_weight.T,
         columns,
         key_side,
     )

time: 79.4 us -> 78.5 us (0.989)
  Pallas kernels: 23.7 us -> 22.8 us
    pallas_call x1, Pallas kernels: 15.8 us -> 15 us  [attend(): pl.pallas_call(attend_kernel, in_specs=[HBM] * (1 + SMALL), out_specs=[VM...]
  transfers between devices with their start and end apart: 6 -> 6, of which waited for: 1 -> 1; matrix products, arithmetic and copies ran while one was open for 0% -> 0% of each run, Pallas kernels for 25% -> 24%
where the time goes in v3:
time: 78.5 us; the launch traced here: 78 us
  blocking collectives  33.1 us (42%)
  Pallas kernels  22.8 us (29%)
  starting transfers between devices  17.5 us (22%)
  waiting for transfers between devices  2.95 us (4%)
  local copies, waits for them, and re-layouts  1.44 us (2%)
    all_to_all x2, blocking collectives, send(): return lax.all_to_all(x, 'col', 0, 0)  31 us
    pallas_call x1, Pallas kernels, attend(): pl.pallas_call(attend_kernel, in_specs=[HBM] * (1 + SMALL), out_specs=[VM...  15 us
    all_to_all x2, starting transfers between devices, send(): return lax.all_to_all(x, 'col', 0, 0)  12.9 us
    ppermute x3, starting transfers between devices, on_device(): lax.ppermute(k_pack, 'row', [(r, (r + 2 * d) % 8) for r in range(8)])  4.55 us
    pallas_call x1, Pallas kernels, key_parts(): pl.pallas_call(key_kernel, in_specs=[HBM] * KEY_SMALL, out_specs=[HBM] *...  4.03 us
    all_to_all x2, waiting for transfers between devices, send(): return lax.all_to_all(x, 'col', 0, 0)  2.93 us
    all_gather x1, blocking collectives, on_device(): lax.all_gather(k_pack, 'row', axis=0, tiled=True, axis_index_groups=cores)  2.11 us
    pallas_call x1, Pallas kernels, pack(): pl.pallas_call(pack_kernel, in_specs=[HBM] * 4, out_specs=[VMEM, VMEM], o...  1.59 us
  transfers between devices with their start and end apart: 6, of which 1 were waited for; matrix products, arithmetic and copies ran while one was open for 0% of the time, Pallas kernels for 24%

profile of v3, /device:TPU:0, one launch (start us, length us, event | category | flops | bytes accessed | tf_op | source)
XLA Modules:
  0.0 78.0 jit_solution(15984757193800943030)
XLA Ops:
  0.0 0.0 copy-start.2
  0.0 0.0 copy-start.1
  0.0 1.6 %shard_map.208 = (bf16[16,24,128]{2,1,0:T(8,128)(2,1)}, bf16[64,512]{1,0:T(8,128)(2,1)}) custom-call(bf16[24,128]{1,0:T(8,128)(2,1)} %bitcast.26, bf16[64,384]{1,0:T(8,128)(2,1)} %ks_in.1, f32[9,64]{1,0:T(8,128)} %krot_in.1, f32[3,64]{1,0:T(4,128)} %kanc_in.1), custom_call_target="tpu_custom_call" | custom-call | tf_op jit(solution)/shard_map/pallas_call | solution.py:416
  1.6 2.1 %all_gather.3.refs_1_ = bf16[128,512]{1,0:T(8,128)(2,1)S(1)} all-gather(bf16[64,512]{1,0:T(8,128)(2,1)} %get-tuple-element.15), channel_id=1, replica_groups={{0,16},{32,48},{64,80},{96,112},{1,17},{33,49},{65,81},{97,113},{2,18},..., dimensions={0}, use_global_device_ids=true | all-gather | bytes 196608 | tf_op jit(solution)/shard_map/all_gather | solution.py:526
  3.7 0.0 copy-start.3
  3.7 2.9 %collective-permute-start.2 = (bf16[128,512]{1,0:T(8,128)(2,1)S(1)}, bf16[128,512]{1,0:T(8,128)(2,1)S(1)}, u32[]{:S(2)}, u32[]{:S(2)}) collective-permute-start(bf16[128,512]{1,0:T(8,128)(2,1)S(1)} %all_gather.3.refs_1_), channel_id=1, source_target_pairs={{0,96},{16,112},{32,0},{48,16},{64,32},{80,48},{96,64},{112,80},{1... | collective-permute-start | bytes 393224 | tf_op jit(solution)/shard_map/ppermute | solution.py:528
  6.6 0.8 %collective-permute-start.1 = (bf16[128,512]{1,0:T(8,128)(2,1)S(1)}, bf16[128,512]{1,0:T(8,128)(2,1)S(1)}, u32[]{:S(2)}, u32[]{:S(2)}) collective-permute-start(bf16[128,512]{1,0:T(8,128)(2,1)S(1)} %all_gather.3.refs_1_), channel_id=1, source_target_pairs={{0,64},{16,80},{32,96},{48,112},{64,0},{80,16},{96,32},{112,48},{1... | collective-permute-start | bytes 393224 | tf_op jit(solution)/shard_map/ppermute | solution.py:528
  7.4 0.9 %collective-permute-start = (bf16[128,512]{1,0:T(8,128)(2,1)S(1)}, bf16[128,512]{1,0:T(8,128)(2,1)S(1)}, u32[]{:S(2)}, u32[]{:S(2)}) collective-permute-start(bf16[128,512]{1,0:T(8,128)(2,1)S(1)} %all_gather.3.refs_1_), channel_id=1, source_target_pairs={{0,32},{16,48},{32,64},{48,80},{64,96},{80,112},{96,0},{112,16},{1... | collective-permute-start | bytes 393224 | tf_op jit(solution)/shard_map/ppermute | solution.py:528
  8.3 8.0 %all-to-all-start = ((bf16[16,24,128]{2,1,0:T(8,128)(2,1)}), bf16[16,24,128]{2,1,0:T(8,128)(2,1)S(1)}, u32[]{:S(2)}, u32[]{:S(2)}) async-start(bf16[16,24,128]{2,1,0:T(8,128)(2,1)} %get-tuple-element.14), calls=%async_computation | async-start | bytes 196608 | tf_op jit(solution)/shard_map/all_to_all | solution.py:522
  16.3 0.0 collective-permute-done.2.refs_4_
  16.3 0.0 copy-start.5
  16.3 0.0 collective-permute-done.1.refs_3_
  16.4 0.0 copy-start.6
  16.4 0.0 collective-permute-done.refs_2_
  16.4 0.0 copy-start.7
  16.4 0.0 copy-done.3
  16.4 0.6 copy-done.5
  17.0 0.1 copy-done.6
  17.0 0.1 copy-done.7
  17.1 4.0 %shard_map.209 = (bf16[16,24,1024]{2,1,0:T(8,128)(2,1)}, bf16[1280,512]{1,0:T(8,128)(2,1)}, f32[96,1280]{1,0:T(8,128)}) custom-call(bf16[24,2016]{1,0:T(8,128)(2,1)} %bitcast.33, bf16[128,512]{1,0:T(8,128)(2,1)} %copy-done.3, bf16[128,512]{1,0:T(8,128)(2,1)} %copy-done.7, bf16[128,512]{1,0:T(8,128)(2,1)} %copy-done.6, bf16[128,512]{1,0:T(8,128)(2,1)} %copy-done.5, ...), custom_call_target="tpu_custom_call" | custom-call | flops 402653184 | bytes 16777216 | tf_op jit(solution)/shard_map/pallas_call | solution.py:434
  21.1 2.9 %all-to-all-done = bf16[16,24,128]{2,1,0:T(8,128)(2,1)S(1)} async-done(((bf16[16,24,128]{2,1,0:T(8,128)(2,1)}), bf16[16,24,128]{2,1,0:T(8,128)(2,1)S(1)}, u32[]{:S(2)}, u32[]{:S(2)}) %all-to-all-start) | async-done | bytes 98336 | tf_op jit(solution)/shard_map/all_to_all | solution.py:522
  24.1 0.0 copy-start.4
  24.1 4.8 %all-to-all-start.1 = ((bf16[16,24,1024]{2,1,0:T(8,128)(2,1)}), bf16[16,24,1024]{2,1,0:T(8,128)(2,1)S(1)}, u32[]{:S(2)}, u32[]{:S(2)}) async-start(bf16[16,24,1024]{2,1,0:T(8,128)(2,1)} %get-tuple-element.19), calls=%async_computation.1 | async-start | bytes 1572864 | tf_op jit(solution)/shard_map/all_to_all | solution.py:522
  28.9 0.0 copy-done.4
  28.9 15.0 %shard_map.210 = (bf16[16,144,128]{2,1,0:T(8,128)(2,1)}, f32[8,512]{1,0:T(8,128)}) custom-call(bf16[128,512,128]{2,1,0:T(8,128)(2,1)} %pair_hbm.1, bf16[12,128]{1,0:T(8,128)(2,1)} %bitcast.34, bf16[384,128]{1,0:T(8,128)(2,1)} %bitcast.25, f32[9,128]{1,0:T(8,128)} %refs_2_.1, f32[3,128]{1,0:T(4,128)} %refs_3_.1, s32[1,128]{1,0:T(1,128)} %bitcast.38, ...), custom_call_target="tpu_custom_call" | custom-call | flops 6442450944 | bytes 50331648 | tf_op jit(solution)/shard_map/pallas_call | solution.py:452
  43.9 0.0 all-to-all-done.1
  43.9 0.1 collective-permute-start.3
  44.0 20.1 %all_to_all.20.refs_0_ = bf16[16,144,128]{2,1,0:T(8,128)(2,1)S(1)} all-to-all(bf16[16,144,128]{2,1,0:T(8,128)(2,1)} %get-tuple-element.20), channel_id=1, replica_groups=mesh['row'=8,'col'=16] {'col'}, dimensions={0} | all-to-all | bytes 1179648 | tf_op jit(solution)/shard_map/all_to_all | solution.py:522
  64.1 0.0 collective-permute-done.3.refs_2_
  64.1 0.0 copy-start
  64.1 0.7 copy-done
  64.9 1.5 %shard_map.211 = f32[16,8,128]{2,1,0:T(8,128)S(1)} custom-call(bf16[16,144,128]{2,1,0:T(8,128)(2,1)S(1)} %all_to_all.20.refs_0_, bf16[384,1024]{1,0:T(8,128)(2,1)S(1)} %bitcast.21, bf16[384,1024]{1,0:T(8,128)(2,1)S(1)} %collective-permute-done.3.refs_2_, f32[8,512]{1,0:T(8,128)S(1)} %copy-done), custom_call_target="tpu_custom_call" | custom-call | tf_op jit(solution)/shard_map/pallas_call | solution.py:474
  66.4 10.9 %all_to_all.21 = f32[16,8,128]{2,1,0:T(8,128)S(1)} all-to-all(f32[16,8,128]{2,1,0:T(8,128)S(1)} %shard_map.211), channel_id=1, replica_groups=mesh['row'=8,'col'=16] {'col'}, dimensions={0} | all-to-all | bytes 131072 | tf_op jit(solution)/shard_map/all_to_all | solution.py:522
  77.3 0.0 copy-done.2
  77.3 0.0 copy-done.1
  77.3 0.7 shard_map.212
Async XLA Ops:
  0.0 77.3 %copy-start.2 = (f32[24]{0:T(128)S(1)}, f32[24]{0:T(128)}, u32[]{:S(2)}) copy-start(f32[24]{0:T(128)} %param.43) | copy-start | bytes 292
  0.0 77.3 %copy-start.1 = (f32[24]{0:T(128)S(1)}, f32[24]{0:T(128)}, u32[]{:S(2)}) copy-start(f32[24]{0:T(128)} %param.42) | copy-start | bytes 292
  3.7 12.7 %copy-start.3 = (bf16[128,512]{1,0:T(8,128)(2,1)}, bf16[128,512]{1,0:T(8,128)(2,1)S(1)}, u32[]{:S(2)}) copy-start(bf16[128,512]{1,0:T(8,128)(2,1)S(1)} %all_gather.3.refs_1_) | copy-start | bytes 393220
  3.7 12.6 %collective-permute-start.2 = (bf16[128,512]{1,0:T(8,128)(2,1)S(1)}, bf16[128,512]{1,0:T(8,128)(2,1)S(1)}, u32[]{:S(2)}, u32[]{:S(2)}) collective-permute-start(bf16[128,512]{1,0:T(8,128)(2,1)S(1)} %all_gather.3.refs_1_), channel_id=1, source_target_pairs={{0,96},{16,112},{32,0},{48,16},{64,32},{80,48},{96,64},{112,80},{1... | collective-permute-start | bytes 393224 | tf_op jit(solution)/shard_map/ppermute | solution.py:528
  6.6 9.8 %collective-permute-start.1 = (bf16[128,512]{1,0:T(8,128)(2,1)S(1)}, bf16[128,512]{1,0:T(8,128)(2,1)S(1)}, u32[]{:S(2)}, u32[]{:S(2)}) collective-permute-start(bf16[128,512]{1,0:T(8,128)(2,1)S(1)} %all_gather.3.refs_1_), channel_id=1, source_target_pairs={{0,64},{16,80},{32,96},{48,112},{64,0},{80,16},{96,32},{112,48},{1... | collective-permute-start | bytes 393224 | tf_op jit(solution)/shard_map/ppermute | solution.py:528
  7.4 9.0 %collective-permute-start = (bf16[128,512]{1,0:T(8,128)(2,1)S(1)}, bf16[128,512]{1,0:T(8,128)(2,1)S(1)}, u32[]{:S(2)}, u32[]{:S(2)}) collective-permute-start(bf16[128,512]{1,0:T(8,128)(2,1)S(1)} %all_gather.3.refs_1_), channel_id=1, source_target_pairs={{0,32},{16,48},{32,64},{48,80},{64,96},{80,112},{96,0},{112,16},{1... | collective-permute-start | bytes 393224 | tf_op jit(solution)/shard_map/ppermute | solution.py:528
  8.3 15.8 %all-to-all-start = ((bf16[16,24,128]{2,1,0:T(8,128)(2,1)}), bf16[16,24,128]{2,1,0:T(8,128)(2,1)S(1)}, u32[]{:S(2)}, u32[]{:S(2)}) async-start(bf16[16,24,128]{2,1,0:T(8,128)(2,1)} %get-tuple-element.14), calls=%async_computation | async-start | bytes 196608 | tf_op jit(solution)/shard_map/all_to_all | solution.py:522
  16.3 0.7 copy-start.5
  16.4 0.7 copy-start.6
  16.4 0.7 copy-start.7
  24.1 4.9 %copy-start.4 = (bf16[16,24,128]{2,1,0:T(8,128)(2,1)}, bf16[16,24,128]{2,1,0:T(8,128)(2,1)S(1)}, u32[]{:S(2)}) copy-start(bf16[16,24,128]{2,1,0:T(8,128)(2,1)S(1)} %all-to-all-done) | copy-start | bytes 294916
  24.1 19.9 %all-to-all-start.1 = ((bf16[16,24,1024]{2,1,0:T(8,128)(2,1)}), bf16[16,24,1024]{2,1,0:T(8,128)(2,1)S(1)}, u32[]{:S(2)}, u32[]{:S(2)}) async-start(bf16[16,24,1024]{2,1,0:T(8,128)(2,1)} %get-tuple-element.19), calls=%async_computation.1 | async-start | bytes 1572864 | tf_op jit(solution)/shard_map/all_to_all | solution.py:522
  43.9 20.2 %collective-permute-start.3 = (bf16[384,1024]{1,0:T(8,128)(2,1)S(1)}, bf16[384,1024]{1,0:T(8,128)(2,1)S(1)}, u32[]{:S(2)}, u32[]{:S(2)}) collective-permute-start(bf16[384,1024]{1,0:T(8,128)(2,1)S(1)} %bitcast.20), channel_id=1, source_target_pairs={{0,16},{16,0},{32,48},{48,32},{64,80},{80,64},{96,112},{112,96},{1... | collective-permute-start | bytes 2359304 | tf_op jit(solution)/shard_map/ppermute | solution.py:561
  64.1 0.7 copy-start

commit v4 on v3

--- a/solution.py
+++ b/solution.py
@@ -110,7 +110,7 @@
     k_out[:, D:] = parts.T.astype(BF16)
     copies[2].wait()
     for c in range(q_out.shape[0]):
-        q_out[c] = qs[...]
+        q_out[c] = qs[...].astype(BF16)
     copies[3].wait()
 
 
@@ -147,12 +147,14 @@
     w, k0, k1, k2, k3, kchain, kw, vw, kpw, vpw, gamma, gap = small
     half = w_pad.shape[1] // 2
     width = w.shape[1]
-    w_pad[:, :width] = w[...]
+    w_pad[:, :width] = w[...].astype(BF16)
     w_pad[:, width:] = jnp.zeros((w.shape[0], 2 * half - width), BF16)
     core = lax.rem(lax.axis_index("row"), 2)
     mine = pl.ds(pl.multiple_of(core * half, half), half)
     cols = w_out.shape[0]
-    stores = fetch_all([(w_pad.at[:, mine], w_out.at[c]) for c in range(cols)], more)
+    half_weights = w_pad[:, mine]
+    for c in range(cols):
+        w_out[c] = half_weights
 
     chips = 4
     here = lax.axis_index("row") // 2
@@ -192,11 +194,7 @@
         by_column = jnp.where(inside, part.astype(F32), by_column)
     columns[:, :DEPTH] = by_column
     columns[:, DEPTH:] = jnp.where(head_row((RB, WIDE)) == value_heads((RB, WIDE)), 1.0, 0.0)
-    stores.append(pltpu.make_async_copy(key_side, key_out, more.at[cols]))
-    stores.append(pltpu.make_async_copy(columns, column_out, more.at[cols + 1]))
-    stores[cols].start()
-    stores[cols + 1].start()
-
+    stores = fetch_all([(key_side, key_out), (columns, column_out)], more)
     for c in stores:
         c.wait()
 
@@ -223,7 +221,7 @@
 
     pick = iota((2 * H, H), 0) - iota((2 * H, H), 1)
     pick = jnp.where((pick == 0) | (pick == H), 1.0, 0.0).astype(BF16)
-    turned = dot(pick, pw[...])
+    turned = dot(pick, pw[...].astype(BF16))
     upper = iota((2 * H, CZ), 0) < H
     weights = jnp.concatenate(
         [jnp.where(upper, turned, 0.0), jnp.where(upper, 0.0, turned)], axis=1
@@ -434,13 +432,13 @@
     return pl.pallas_call(
         key_kernel,
         in_specs=[HBM] * KEY_SMALL,
-        out_specs=[HBM] * 3,
+        out_specs=[VMEM, HBM, HBM],
         out_shape=results,
         scratch_shapes=held((out_weight,) + small)
         + [pltpu.VMEM((width, 2 * HALF), BF16)]
         + held(results[1:])
-        + [pltpu.VMEM((keys, D + 128), BF16), signals(KEY_SMALL), signals(2 + cols)],
-        compiler_params=PARAMS,
+        + [pltpu.VMEM((keys, D + 128), BF16), signals(KEY_SMALL), signals(2)],
+        compiler_params=pltpu.CompilerParams(vmem_limit_bytes=VMEM_BYTES - 1_000_000),
         cost_estimate=pl.CostEstimate(
             flops=2 * D * keys * 1024, bytes_accessed=16 << 20, transcendentals=0
         ),
@@ -521,7 +519,7 @@
     def send(x):
         return lax.all_to_all(x, "col", 0, 0)
 
-    q_pack, k_pack = pack(cols, query_single.T, key_single, key_rotation, key_anchor)
+    q_pack, k_pack = pack(cols, query_single.T.astype(F32), key_single, key_rotation, key_anchor)
     cores = [[2 * x, 2 * x + 1] for x in range(4)]
     k_pack = lax.all_gather(k_pack, "row", axis=0, tiled=True, axis_index_groups=cores)
     k_others = [
@@ -531,7 +529,7 @@
     gamma = head_gamma.reshape(1, -1)
     w_pack, key_side, columns = key_parts(
         cols,
-        out_weight.T,
+        out_weight.T.astype(F32),
         k_pack,
         *k_others,
         key_chain.reshape(1, -1),
@@ -545,7 +543,7 @@
     weights = send(w_pack).reshape(D, HALF)
     parts, aux = attend(
         pair_tile,
-        pair_weight.T,
+        pair_weight.T.astype(F32),
         qall,
         query_rotation,
         query_anchor,

time: 78.5 us -> 84.1 us (1.071)
  other arithmetic: 0 us -> 4.18 us
  starting transfers between devices: 17.5 us -> 20.5 us
  waiting for transfers between devices: 2.95 us -> 0.69 us
    convert_element_type x0 -> x3, other arithmetic: none -> 4.18 us  [the longest x1 1.58 us: on_device(): out_weight.T.astype(F32)]
    all_to_all x2, waiting for transfers between devices: 2.93 us -> 0.68 us  [send(): return lax.all_to_all(x, 'col', 0, 0)]
    all_to_all x2, starting transfers between devices: 12.9 us -> 14.6 us  [send(): return lax.all_to_all(x, 'col', 0, 0)]
    ppermute x3, starting transfers between devices: 4.55 us -> 5.76 us  [on_device(): lax.ppermute(k_pack, 'row', [(r, (r + 2 * d) % 8) for r in range(8)])]
  transfers between devices with their start and end apart: 6 -> 6, of which waited for: 1 -> 1; matrix products, arithmetic and copies ran while one was open for 0% -> 3% of each run, Pallas kernels for 24% -> 24%
where the time goes in v4:
time: 84.1 us; the launch traced here: 83.5 us
  blocking collectives  33.1 us (39%)
  Pallas kernels  23.5 us (28%)
  starting transfers between devices  20.5 us (24%)
  other arithmetic  4.18 us (5%)
  local copies, waits for them, and re-layouts  1.46 us (2%)
    all_to_all x2, blocking collectives, send(): return lax.all_to_all(x, 'col', 0, 0)  31 us
    pallas_call x1, Pallas kernels, attend(): pl.pallas_call(attend_kernel, in_specs=[HBM] * (1 + SMALL), out_specs=[VM...  15 us
    all_to_all x2, starting transfers between devices, send(): return lax.all_to_all(x, 'col', 0, 0)  14.6 us
    ppermute x3, starting transfers between devices, on_device(): lax.ppermute(k_pack, 'row', [(r, (r + 2 * d) % 8) for r in range(8)])  5.76 us
    pallas_call x1, Pallas kernels, key_parts(): pl.pallas_call(key_kernel, in_specs=[HBM] * KEY_SMALL, out_specs=[VMEM, H...  4.71 us
    all_gather x1, blocking collectives, on_device(): lax.all_gather(k_pack, 'row', axis=0, tiled=True, axis_index_groups=cores)  2.11 us
  transfers between devices with their start and end apart: 6, of which 1 were waited for; matrix products, arithmetic and copies ran while one was open for 3% of the time, Pallas kernels for 24%

profile of v4, /device:TPU:0, one launch (start us, length us, event | category | flops | bytes accessed | tf_op | source)
XLA Modules:
  0.0 83.5 jit_solution(16822706959232244173)
XLA Ops:
  0.0 0.0 copy-start.1
  0.0 0.0 copy-start.2
  0.0 1.3 %convert_bitcast_fusion.1.qs_in = f32[24,128]{1,0:T(8,128)} fusion(bf16[128,24]{0,1:T(8,128)(2,1)} %param.22), kind=kLoop, calls=%fused_computation.1 | loop fusion | flops 3072 | bytes 18432 | tf_op jit(solution)/shard_map/convert_element_type | solution.py:522
  1.3 1.6 %shard_map.208 = (bf16[16,24,128]{2,1,0:T(8,128)(2,1)}, bf16[64,512]{1,0:T(8,128)(2,1)}) custom-call(f32[24,128]{1,0:T(8,128)} %convert_bitcast_fusion.1.qs_in, bf16[64,384]{1,0:T(8,128)(2,1)} %ks_in.1, f32[9,64]{1,0:T(8,128)} %krot_in.1, f32[3,64]{1,0:T(4,128)} %kanc_in.1), custom_call_target="tpu_custom_call" | custom-call | tf_op jit(solution)/shard_map/pallas_call | solution.py:414
  2.9 2.1 %all_gather.3.refs_1_ = bf16[128,512]{1,0:T(8,128)(2,1)S(1)} all-gather(bf16[64,512]{1,0:T(8,128)(2,1)} %get-tuple-element.15), channel_id=1, replica_groups={{0,16},{32,48},{64,80},{96,112},{1,17},{33,49},{65,81},{97,113},{2,18},..., dimensions={0}, use_global_device_ids=true | all-gather | bytes 196608 | tf_op jit(solution)/shard_map/all_gather | solution.py:524
  5.0 0.0 copy-start.3
  5.0 1.6 %collective-permute-start = (bf16[128,512]{1,0:T(8,128)(2,1)S(1)}, bf16[128,512]{1,0:T(8,128)(2,1)S(1)}, u32[]{:S(2)}, u32[]{:S(2)}) collective-permute-start(bf16[128,512]{1,0:T(8,128)(2,1)S(1)} %all_gather.3.refs_1_), channel_id=1, source_target_pairs={{0,32},{16,48},{32,64},{48,80},{64,96},{80,112},{96,0},{112,16},{1... | collective-permute-start | bytes 393224 | tf_op jit(solution)/shard_map/ppermute | solution.py:526
  6.6 2.7 %collective-permute-start.1 = (bf16[128,512]{1,0:T(8,128)(2,1)S(1)}, bf16[128,512]{1,0:T(8,128)(2,1)S(1)}, u32[]{:S(2)}, u32[]{:S(2)}) collective-permute-start(bf16[128,512]{1,0:T(8,128)(2,1)S(1)} %all_gather.3.refs_1_), channel_id=1, source_target_pairs={{0,64},{16,80},{32,96},{48,112},{64,0},{80,16},{96,32},{112,48},{1... | collective-permute-start | bytes 393224 | tf_op jit(solution)/shard_map/ppermute | solution.py:526
  9.3 1.4 %collective-permute-start.2 = (bf16[128,512]{1,0:T(8,128)(2,1)S(1)}, bf16[128,512]{1,0:T(8,128)(2,1)S(1)}, u32[]{:S(2)}, u32[]{:S(2)}) collective-permute-start(bf16[128,512]{1,0:T(8,128)(2,1)S(1)} %all_gather.3.refs_1_), channel_id=1, source_target_pairs={{0,96},{16,112},{32,0},{48,16},{64,32},{80,48},{96,64},{112,80},{1... | collective-permute-start | bytes 393224 | tf_op jit(solution)/shard_map/ppermute | solution.py:526
  10.8 8.0 %all-to-all-start = ((bf16[16,24,128]{2,1,0:T(8,128)(2,1)}), bf16[16,24,128]{2,1,0:T(8,128)(2,1)S(1)}, u32[]{:S(2)}, u32[]{:S(2)}) async-start(bf16[16,24,128]{2,1,0:T(8,128)(2,1)} %get-tuple-element.14), calls=%async_computation | async-start | bytes 196608 | tf_op jit(solution)/shard_map/all_to_all | solution.py:520
  18.8 1.6 %convert_bitcast_fusion.refs_0_ = f32[24,2016]{1,0:T(8,128)} fusion(bf16[2016,24]{0,1:T(8,128)(2,1)} %param.41), kind=kLoop, calls=%fused_computation | loop fusion | flops 48384 | bytes 290304 | tf_op jit(solution)/shard_map/convert_element_type | solution.py:532
  20.4 0.0 collective-permute-done.refs_2_
  20.4 0.0 copy-start.5
  20.4 0.0 collective-permute-done.1.refs_3_
  20.4 0.0 copy-start.6
  20.4 0.0 collective-permute-done.2.refs_4_
  20.5 0.0 copy-start.7
  20.5 0.0 copy-done.3
  20.5 0.6 copy-done.5
  21.1 0.0 copy-done.6
  21.1 0.1 copy-done.7
  21.2 4.7 %shard_map.209 = (bf16[16,24,1024]{2,1,0:T(8,128)(2,1)}, bf16[1280,512]{1,0:T(8,128)(2,1)}, f32[96,1280]{1,0:T(8,128)}) custom-call(f32[24,2016]{1,0:T(8,128)} %convert_bitcast_fusion.refs_0_, bf16[128,512]{1,0:T(8,128)(2,1)} %copy-done.3, bf16[128,512]{1,0:T(8,128)(2,1)} %copy-done.5, bf16[128,512]{1,0:T(8,128)(2,1)} %copy-done.6, ...), custom_call_target="tpu_custom_call" | custom-call | flops 402653184 | bytes 16777216 | tf_op jit(solution)/shard_map/pallas_call | solution.py:432
  25.9 0.7 all-to-all-done
  26.6 0.0 copy-start.4
  26.6 6.6 %all-to-all-start.1 = ((bf16[16,24,1024]{2,1,0:T(8,128)(2,1)}), bf16[16,24,1024]{2,1,0:T(8,128)(2,1)S(1)}, u32[]{:S(2)}, u32[]{:S(2)}) async-start(bf16[16,24,1024]{2,1,0:T(8,128)(2,1)} %get-tuple-element.19), calls=%async_computation.1 | async-start | bytes 1572864 | tf_op jit(solution)/shard_map/all_to_all | solution.py:520
  33.2 1.3 %convert_bitcast_fusion.2.refs_0_ = f32[12,128]{1,0:T(8,128)} fusion(bf16[128,12]{0,1:T(8,128)(2,1)} %param.38), kind=kLoop, calls=%fused_computation.2 | loop fusion | flops 1536 | bytes 9216 | tf_op jit(solution)/shard_map/convert_element_type | solution.py:546
  34.4 0.0 copy-done.4
  34.4 15.0 %shard_map.210 = (bf16[16,144,128]{2,1,0:T(8,128)(2,1)}, f32[8,512]{1,0:T(8,128)}) custom-call(bf16[128,512,128]{2,1,0:T(8,128)(2,1)} %pair_hbm.1, f32[12,128]{1,0:T(8,128)} %convert_bitcast_fusion.2.refs_0_, bf16[384,128]{1,0:T(8,128)(2,1)} %bitcast.28, f32[9,128]{1,0:T(8,128)} %refs_2_.1, f32[3,128]{1,0:T(4,128)} %refs_3_.1, s32[1,128]{1,0:T(1,128)} %bitcast.38, ...), custom_call_target="tpu_custom_call" | custom-call | flops 6442450944 | bytes 50331648 | tf_op jit(solution)/shard_map/pallas_call | solution.py:450
  49.4 0.0 all-to-all-done.1
  49.4 0.1 collective-permute-start.3
  49.5 20.1 %all_to_all.20.refs_0_ = bf16[16,144,128]{2,1,0:T(8,128)(2,1)S(1)} all-to-all(bf16[16,144,128]{2,1,0:T(8,128)(2,1)} %get-tuple-element.20), channel_id=1, replica_groups=mesh['row'=8,'col'=16] {'col'}, dimensions={0} | all-to-all | bytes 1179648 | tf_op jit(solution)/shard_map/all_to_all | solution.py:520
  69.6 0.0 collective-permute-done.3.refs_2_
  69.6 0.0 copy-start
  69.6 0.7 copy-done
  70.4 1.5 %shard_map.211 = f32[16,8,128]{2,1,0:T(8,128)S(1)} custom-call(bf16[16,144,128]{2,1,0:T(8,128)(2,1)S(1)} %all_to_all.20.refs_0_, bf16[384,1024]{1,0:T(8,128)(2,1)S(1)} %bitcast.24, bf16[384,1024]{1,0:T(8,128)(2,1)S(1)} %collective-permute-done.3.refs_2_, f32[8,512]{1,0:T(8,128)S(1)} %copy-done), custom_call_target="tpu_custom_call" | custom-call | tf_op jit(solution)/shard_map/pallas_call | solution.py:472
  71.9 10.9 %all_to_all.21 = f32[16,8,128]{2,1,0:T(8,128)S(1)} all-to-all(f32[16,8,128]{2,1,0:T(8,128)S(1)} %shard_map.211), channel_id=1, replica_groups=mesh['row'=8,'col'=16] {'col'}, dimensions={0} | all-to-all | bytes 131072 | tf_op jit(solution)/shard_map/all_to_all | solution.py:520
  82.8 0.0 copy-done.1
  82.8 0.0 copy-done.2
  82.8 0.7 shard_map.212
Async XLA Ops:
  0.0 82.8 %copy-start.1 = (f32[24]{0:T(128)S(1)}, f32[24]{0:T(128)}, u32[]{:S(2)}) copy-start(f32[24]{0:T(128)} %param.42) | copy-start | bytes 292
  0.0 82.8 %copy-start.2 = (f32[24]{0:T(128)S(1)}, f32[24]{0:T(128)}, u32[]{:S(2)}) copy-start(f32[24]{0:T(128)} %param.43) | copy-start | bytes 292
  5.0 15.5 %copy-start.3 = (bf16[128,512]{1,0:T(8,128)(2,1)}, bf16[128,512]{1,0:T(8,128)(2,1)S(1)}, u32[]{:S(2)}) copy-start(bf16[128,512]{1,0:T(8,128)(2,1)S(1)} %all_gather.3.refs_1_) | copy-start | bytes 393220
  5.0 15.4 %collective-permute-start = (bf16[128,512]{1,0:T(8,128)(2,1)S(1)}, bf16[128,512]{1,0:T(8,128)(2,1)S(1)}, u32[]{:S(2)}, u32[]{:S(2)}) collective-permute-start(bf16[128,512]{1,0:T(8,128)(2,1)S(1)} %all_gather.3.refs_1_), channel_id=1, source_target_pairs={{0,32},{16,48},{32,64},{48,80},{64,96},{80,112},{96,0},{112,16},{1... | collective-permute-start | bytes 393224 | tf_op jit(solution)/shard_map/ppermute | solution.py:526
  6.6 13.8 %collective-permute-start.1 = (bf16[128,512]{1,0:T(8,128)(2,1)S(1)}, bf16[128,512]{1,0:T(8,128)(2,1)S(1)}, u32[]{:S(2)}, u32[]{:S(2)}) collective-permute-start(bf16[128,512]{1,0:T(8,128)(2,1)S(1)} %all_gather.3.refs_1_), channel_id=1, source_target_pairs={{0,64},{16,80},{32,96},{48,112},{64,0},{80,16},{96,32},{112,48},{1... | collective-permute-start | bytes 393224 | tf_op jit(solution)/shard_map/ppermute | solution.py:526
  9.3 11.1 %collective-permute-start.2 = (bf16[128,512]{1,0:T(8,128)(2,1)S(1)}, bf16[128,512]{1,0:T(8,128)(2,1)S(1)}, u32[]{:S(2)}, u32[]{:S(2)}) collective-permute-start(bf16[128,512]{1,0:T(8,128)(2,1)S(1)} %all_gather.3.refs_1_), channel_id=1, source_target_pairs={{0,96},{16,112},{32,0},{48,16},{64,32},{80,48},{96,64},{112,80},{1... | collective-permute-start | bytes 393224 | tf_op jit(solution)/shard_map/ppermute | solution.py:526
  10.8 15.8 %all-to-all-start = ((bf16[16,24,128]{2,1,0:T(8,128)(2,1)}), bf16[16,24,128]{2,1,0:T(8,128)(2,1)S(1)}, u32[]{:S(2)}, u32[]{:S(2)}) async-start(bf16[16,24,128]{2,1,0:T(8,128)(2,1)} %get-tuple-element.14), calls=%async_computation | async-start | bytes 196608 | tf_op jit(solution)/shard_map/all_to_all | solution.py:520
  20.4 0.7 copy-start.5
  20.4 0.7 copy-start.6
  20.5 0.7 copy-start.7
  26.6 7.9 %copy-start.4 = (bf16[16,24,128]{2,1,0:T(8,128)(2,1)}, bf16[16,24,128]{2,1,0:T(8,128)(2,1)S(1)}, u32[]{:S(2)}) copy-start(bf16[16,24,128]{2,1,0:T(8,128)(2,1)S(1)} %all-to-all-done) | copy-start | bytes 294916
  26.6 22.9 %all-to-all-start.1 = ((bf16[16,24,1024]{2,1,0:T(8,128)(2,1)}), bf16[16,24,1024]{2,1,0:T(8,128)(2,1)S(1)}, u32[]{:S(2)}, u32[]{:S(2)}) async-start(bf16[16,24,1024]{2,1,0:T(8,128)(2,1)} %get-tuple-element.19), calls=%async_computation.1 | async-start | bytes 1572864 | tf_op jit(solution)/shard_map/all_to_all | solution.py:520
  49.4 20.2 %collective-permute-start.3 = (bf16[384,1024]{1,0:T(8,128)(2,1)S(1)}, bf16[384,1024]{1,0:T(8,128)(2,1)S(1)}, u32[]{:S(2)}, u32[]{:S(2)}) collective-permute-start(bf16[384,1024]{1,0:T(8,128)(2,1)S(1)} %bitcast.23), channel_id=1, source_target_pairs={{0,16},{16,0},{32,48},{48,32},{64,80},{80,64},{96,112},{112,96},{1... | collective-permute-start | bytes 2359304 | tf_op jit(solution)/shard_map/ppermute | solution.py:559
  69.6 0.7 copy-start
